TPU v7x, 32 devices: a whole 2x2x4 slice. The times are simulated.
32 devices in a mesh: grp: 2 (over x), vir: 16 (over z, y, core).
Axes of the slice: x: 2, y: 2, z: 4, core: 2. Of those that a mesh axis runs over, the one named last changes fastest.
Arguments:
- amplitudes: bfloat16 [32, 1024, 1024], P(('grp', 'vir')), parts along dimension 0, may hold values from -6 to 6
- couplings: bfloat16 [4096, 16, 2048], P(('grp', 'vir')), parts along dimension 0, may hold values from -0.125 to 0.125
- occ_irrep: int32 [32], P('grp'), parts along dimension 0, may hold values from 0 to 7
- pair_irrep: int32 [1], replicated, may hold values from 0 to 7
- j_irrep: int32 [2], replicated, may hold values from 0 to 7
- block_sizes: int32 [16], P('grp'), parts along dimension 0, may hold values from 1 to 256, 1024 in all
- owner: int32 [512, 1], P('grp'), parts along dimension 0, may hold values from 0 to 15; in each aligned block of 256 rows (0 to 255, 256 to 511, ...) at most 32 rows name the same one
Outputs:
- cycle: float32 [2048, 2048], P(('grp', 'vir')), parts along dimension 0
There are 2 independent parts, one for each index of `grp`. A program takes and returns all parts, laid end to end along the dimension named above; an argument that names none is the same for every part. Nothing has to cross between parts.
Inputs may be any that keep to these rules, and one draw needn't show every extreme that they name: `block_sizes`: the eight blocks are consecutive in virtual order and sum to 1024; the largest holds exactly 256 virtuals. `owner`: no device owns more than 32 blocks, and some device owns exactly 32.
All inputs are finite; a program needn't handle non-finite values.
Results may differ from a plain program's by a relative error of at most 0.0003.
Values may be sent and summed in bfloat16 or wider, within the bound.
No kernel may reach another device: no remote copies, remote signals or barrier semaphores. Data moves between devices by JAX's collectives and lax.ppermute only.
A program may use at most 128 MiB of HBM per device.

v0:
```python
import jax
import jax.numpy as jnp
from jax import lax
from jax.sharding import PartitionSpec as P

BS = 4


def per_device(amplitudes, couplings, occ_irrep, pair_irrep, j_irrep, block_sizes, owner):
    devices = lax.axis_size("vir")
    my_index = lax.axis_index("vir")
    m_local = amplitudes.shape[0]
    virt_count = amplitudes.shape[2]
    slots_dev = couplings.shape[0]
    cap_slots = slots_dev // BS
    block_count = owner.shape[0]
    columns = couplings.shape[2]
    ends = jnp.cumsum(block_sizes)
    virtual = jnp.arange(virt_count, dtype=jnp.int32)
    labels = jnp.sum((virtual[:, None] >= ends[None, :]).astype(jnp.int32), axis=1)
    owners = owner[:, 0]
    blocks = jnp.arange(block_count, dtype=jnp.int32)
    same_owner = owners[:, None] == owners[None, :]
    earlier = blocks[None, :] < blocks[:, None]
    ranking = jnp.sum((same_owner & earlier).astype(jnp.int32), axis=1)
    slot_index = owners * cap_slots + ranking
    slot_ids = jnp.arange(devices * cap_slots, dtype=jnp.int32)
    matches = slot_index[None, :] == slot_ids[:, None]
    block_of = jnp.sum(jnp.where(matches, blocks[None, :], 0), axis=1)
    filled = jnp.any(matches, axis=1)
    within = jnp.arange(BS, dtype=jnp.int32)
    e_index = (block_of[:, None] * BS + within[None, :]).reshape(devices * cap_slots * BS)
    e_filled = jnp.broadcast_to(filled[:, None], (devices * cap_slots, BS)).reshape(
        devices * cap_slots * BS
    )
    occ_local = lax.dynamic_slice_in_dim(occ_irrep, my_index * m_local, m_local)
    wanted = jnp.bitwise_xor(pair_irrep[0], occ_local)
    my_e = lax.dynamic_slice_in_dim(e_index, my_index * slots_dev, slots_dev)
    label_e = jnp.take(labels, my_e)
    t_allowed = jnp.bitwise_xor(labels[:, None], labels[None, :])[None] == wanted[:, None, None]
    masked_t = jnp.where(t_allowed, amplitudes, jnp.zeros((), amplitudes.dtype))
    outgoing = jnp.take(masked_t, e_index, axis=1)
    outgoing = jnp.where(e_filled[None, :, None], outgoing, jnp.zeros((), outgoing.dtype))
    received = lax.all_to_all(outgoing, "vir", split_axis=1, concat_axis=0, tiled=True)
    column_irrep = jnp.bitwise_xor(labels[:, None], j_irrep[None, :]).reshape(columns)
    w_allowed = (
        jnp.bitwise_xor(label_e[:, None], occ_irrep[None, :])[:, :, None]
        == column_irrep[None, None, :]
    )
    masked_w = jnp.where(w_allowed, couplings, jnp.zeros((), couplings.dtype))
    return lax.psum_scatter(
        lax.dot_general(
            received, masked_w, (((0, 1), (1, 0)), ((), ())), preferred_element_type=jnp.float32
        ),
        "vir",
        scatter_dimension=0,
        tiled=True,
    )


def solution(mesh):
    return jax.shard_map(
        per_device,
        mesh=mesh,
        in_specs=(
            P(("grp", "vir"), None, None),
            P(("grp", "vir"), None, None),
            P("grp"),
            P(),
            P(),
            P("grp"),
            P("grp", None),
        ),
        out_specs=P(("grp", "vir"), None),
        check_vma=False,
    )
```

profile of v0, /device:TPU:0, one launch (start us, length us, event | category | flops | bytes accessed | tf_op | source)
XLA Modules:
  0.0 343.0 jit_solution(4185014565158207086)
XLA Ops:
  6.5 0.9 convert_reduce_fusion
  7.5 0.7 multiply_add_fusion
  8.2 0.2 fusion.8
  8.3 0.2 select_reduce_fusion
  8.5 0.1 iota_add_fusion
  8.6 0.2 add.77
  8.8 0.2 add.81
  9.6 0.8 reduce-window.8
  10.4 0.1 convert_reduce_fusion.1
  10.5 0.1 broadcast_in_dim.76
  10.7 0.2 broadcast_in_dim.77
  10.9 1.2 dynamic_slice.6
  12.8 2.3 fusion.7
  15.1 9.7 %gather_fusion = bf16[2048,1024]{1,0:T(8,128)(2,1)} fusion(bf16[1024,1024]{1,0:T(8,128)(2,1)S(1)} %fusion.7, s32[2048]{0:T(1024)S(1)} %broadcast_clamp_fusion), kind=kCustom, calls=%fused_computation | custom fusion | bytes 8396800 | tf_op jit(solution)/shard_map/jit(_take)/gather | solution.py:42
  24.8 2.6 fusion.5
  27.4 28.7 %copy.24 = bf16[1,2048,1024]{2,0,1:T(2,128)(2,1)} copy(bf16[1,2048,1024]{2,1,0:T(8,128)(2,1)S(1)} %fusion.5) | data formatting | bytes 8388608 | tf_op jit(solution)/shard_map/jit(_where)/select_n | solution.py:43
  56.1 0.5 broadcast.167
  56.6 26.0 %reduce = bf16[2048,1024]{1,0:T(8,128)(2,1)} reduce(bf16[2048,1,1024]{2,1,0:T(2,128)(2,1)} %bitcast.19, bf16[]{:T(256)} %broadcast.167), dimensions={1}, to_apply=%bitcast.18.reduce_sub_computation | reduce | bytes 8388610
  82.6 11.4 %reshape.260 = bf16[16,2,65536]{2,1,0:T(2,128)(2,1)} reshape(bf16[2048,1024]{1,0:T(8,128)(2,1)} %reduce) | data formatting | bytes 8388608
  93.9 0.0 copy-start.1
  93.9 0.0 copy-start.2
  94.0 7.6 %all-to-all-start = ((bf16[16,2,65536]{2,1,0:T(2,128)(2,1)}), bf16[16,2,65536]{2,1,0:T(2,128)(2,1)}, u32[]{:S(2)}, u32[]{:S(2)}) async-start(bf16[16,2,65536]{2,1,0:T(2,128)(2,1)} %reshape.260), calls=%async_computation | async-start | bytes 8388608 | tf_op jit(solution)/shard_map/all_to_all | solution.py:44
  101.5 0.2 reduce-scatter.2.cloned.1.call-start
  101.8 0.1 compare_select_fusion.3
  101.9 1.0 gather_fusion.1
  102.8 0.0 copy-done.1
  102.8 0.2 broadcast_xor_fusion
  103.0 0.3 xor.70
  103.3 0.1 and_select_fusion
  103.4 0.0 copy-done.2
  103.4 0.1 broadcast_xor_fusion.1
  103.5 7.8 %compare_select_fusion = bf16[128,16,2048]{2,1,0:T(8,128)(2,1)} fusion(bf16[128,16,2048]{2,1,0:T(8,128)(2,1)} %param.8, s32[2048]{0:T(1024)S(1)} %xor.70, s32[128,16]{1,0:T(8,128)S(1)} %broadcast_xor_fusion.1), kind=kLoop, calls=%fused_computation.2 | loop fusion | flops 8388608 | bytes 16793600 | tf_op jit(solution)/shard_map/jit(_where)/select_n | solution.py:50
  111.3 67.9 %all-to-all-done = bf16[16,2,65536]{2,1,0:T(2,128)(2,1)} async-done(((bf16[16,2,65536]{2,1,0:T(2,128)(2,1)}), bf16[16,2,65536]{2,1,0:T(2,128)(2,1)}, u32[]{:S(2)}, u32[]{:S(2)}) %all-to-all-start) | async-done | bytes 4194336 | tf_op jit(solution)/shard_map/all_to_all | solution.py:44
  179.2 12.4 %reshape.261 = bf16[2048,1,1024]{2,1,0:T(2,128)(2,1)} reshape(bf16[16,2,65536]{2,1,0:T(2,128)(2,1)} %all-to-all-done) | data formatting | bytes 8388608
  191.6 0.0 copy-start
  191.6 5.3 %copy.18 = bf16[1,2048,1024]{2,1,0:T(8,128)(2,1)S(1)} copy(bf16[1,2048,1024]{2,0,1:T(2,128)(2,1)} %bitcast.20) | data formatting | bytes 8388608
  196.9 0.5 copy-done
  197.4 19.0 %fusion.2 = f32[1024,2048]{1,0:T(8,128)} fusion(bf16[16,128,1024]{2,1,0:T(8,128)(2,1)S(1)} %bitcast.21, bf16[128,16,2048]{2,1,0:T(8,128)(2,1)S(1)} %copy-done), kind=kOutput, calls=%fused_computation.5 | convolution fusion | flops 8589934592 | bytes 20971520 | tf_op jit(solution)/shard_map/dot_general | solution.py:52
  216.4 0.0 reduce-scatter.2.cloned.1.call-update
  216.4 119.7 %reduce-scatter.2.cloned.1.call-done = f32[64,2048]{1,0:T(8,128)} async-done(((f32[1024,2048]{1,0:T(8,128)}), f32[64,2048]{1,0:T(8,128)}) %reduce-scatter.2.cloned.1.call-update) | async-done | bytes 524304 | tf_op jit(solution)/shard_map/reduce_scatter | solution.py:51
  (5 shorter events, 0.0 us)
Async XLA Ops:
  93.9 8.9 %copy-start.1 = (s32[2]{0:T(128)S(1)}, s32[2]{0:T(128)}, u32[]{:S(2)}) copy-start(s32[2]{0:T(128)} %param.11) | copy-start | bytes 28
  93.9 9.4 %copy-start.2 = (s32[16]{0:T(128)S(1)}, s32[16]{0:T(128)}, u32[]{:S(2)}) copy-start(s32[16]{0:T(128)} %param.9) | copy-start | bytes 196
  94.0 85.3 %all-to-all-start = ((bf16[16,2,65536]{2,1,0:T(2,128)(2,1)}), bf16[16,2,65536]{2,1,0:T(2,128)(2,1)}, u32[]{:S(2)}, u32[]{:S(2)}) async-start(bf16[16,2,65536]{2,1,0:T(2,128)(2,1)} %reshape.260), calls=%async_computation | async-start | bytes 8388608 | tf_op jit(solution)/shard_map/all_to_all | solution.py:44
  101.5 234.6 %reduce-scatter.2.cloned.1.call-start = ((), (), s32[]{:S(2)}) async-start(), calls=%async_computation.2 | async-start | bytes 8912896 | tf_op jit(solution)/shard_map/reduce_scatter | solution.py:51
  191.6 5.8 %copy-start = (bf16[128,16,2048]{2,1,0:T(8,128)(2,1)S(1)}, bf16[128,16,2048]{2,1,0:T(8,128)(2,1)}, u32[]{:S(2)}) copy-start(bf16[128,16,2048]{2,1,0:T(8,128)(2,1)} %compare_select_fusion) | copy-start | bytes 25165828
Sparse Core Ops, SparseCore 0:
  216.5 119.5 reduce-scatter.1
where the time goes:
time: 344 us; the launch traced here: 343 us
  waiting for transfers between devices  188 us (55%)
  local copies, waits for them, and re-layouts  71.6 us (21%)
  other arithmetic  42.1 us (12%)
  matrix products  19 us (6%)
  between operations  14.8 us (4%)
  starting transfers between devices  7.79 us (2%)
    reduce_scatter x1, waiting for transfers between devices, per_device(): lax.psum_scatter(lax.dot_general(received, masked_w, (((0, 1), (1, 0)), (...  120 us
    all_to_all x1, waiting for transfers between devices, per_device(): lax.all_to_all(outgoing, 'vir', split_axis=1, concat_axis=0, tiled=True)  67.9 us
    unnamed x10, local copies, waits for them, and re-layouts  30.1 us
    select_n x1, local copies, waits for them, and re-layouts, per_device(): jnp.where(e_filled[None, :, None], outgoing, jnp.zeros((), outgoing.dtype))  28.7 us
    unnamed x1, other arithmetic  26 us
    dot_general x1, matrix products, per_device(): lax.dot_general(received, masked_w, (((0, 1), (1, 0)), ((), ())), preferr...  19 us
    gather x1, local copies, waits for them, and re-layouts, per_device(): outgoing = jnp.take(masked_t, e_index, axis=1)  9.67 us
    select_n x1, other arithmetic, per_device(): masked_w = jnp.where(w_allowed, couplings, jnp.zeros((), couplings.dtype))  7.8 us
  transfers between devices with their start and end apart: 2, of which 2 were waited for; matrix products, arithmetic and copies ran while one was open for 3% of the time, Pallas kernels for 0%

commit v1 on v0

v1 whole, which is shorter than its diff:
```python
import functools

import jax
import jax.numpy as jnp
from jax import lax
from jax.experimental import pallas as pl
from jax.experimental.pallas import tpu as pltpu
from jax.sharding import PartitionSpec as P

BS = 4
MOST = 256
LIMIT = 48 * 1024 * 1024
F32, BF16, I32 = jnp.float32, jnp.bfloat16, jnp.int32


def irrep_of(index, sizes):
    label = jnp.zeros_like(index)
    end = jnp.int32(0)
    for h in range(sizes.shape[0]):
        end = end + sizes[h]
        label = label + (index >= end).astype(I32)
    return label


def iota(shape, dim):
    return lax.broadcasted_iota(I32, shape, dim)


def column_keys(columns, sizes, j_irrep):
    count = j_irrep.shape[0]
    column = iota((1, columns), 1)
    j = column % count
    j_label = jnp.zeros_like(column)
    for i in range(count):
        j_label = jnp.where(j == i, j_irrep[i], j_label)
    return irrep_of(column // count, sizes) ^ j_label


def coupling_row(owner_row, virtuals, rows):
    blocks = owner_row.shape[1]
    first, second = iota((blocks, blocks), 0), iota((blocks, blocks), 1)
    owner_col = jnp.sum(jnp.where(first == second, owner_row, 0), axis=1, keepdims=True)
    earlier = (owner_col == owner_row) & (first < second)
    rank = jnp.sum(earlier.astype(I32), axis=0, keepdims=True)
    place = owner_row * rows + rank * BS
    e, block = iota((virtuals, blocks), 0), iota((virtuals, blocks), 1)
    start = jnp.sum(jnp.where(e // BS == block, place, 0), axis=1, keepdims=True)
    return start + iota((virtuals, 1), 0) % BS


def pack_kernel(
    rows, rows_out, sizes, occ, pair, owner_row, t_hbm, out, t_vmem, folded_t, target, sem
):
    virtuals = t_hbm.shape[1]
    lanes = 2 * rows

    @pl.when(pl.program_id(0) == 0)
    def _():
        copy = pltpu.make_async_copy(t_hbm.at[0], t_vmem, sem)
        copy.start()
        target[...] = jnp.broadcast_to(
            coupling_row(owner_row[...], virtuals, rows), target.shape
        )
        wanted = pair[0] ^ occ[lax.axis_index("vir")]
        label_e = irrep_of(iota((virtuals, 1), 0), sizes) ^ wanted
        label_a = irrep_of(iota((1, virtuals), 1), sizes)
        copy.wait()
        folded = jnp.zeros((virtuals, MOST), F32)
        for k in range(virtuals // MOST):
            part = slice(k * MOST, (k + 1) * MOST)
            folded = folded + jnp.where(
                label_e == label_a[:, part], t_vmem[:, part].astype(F32), 0.0
            )
        folded_t[...] = folded.T.astype(BF16)

    chips = out.shape[0] // 2
    for chip in range(chips):
        lane = iota((virtuals, lanes), 1)
        offset = (pl.program_id(0) * chips + chip) * lanes
        place = target[:, :1] - offset

        def moved(flip):
            hot = jnp.where(place == lane ^ flip, 1.0, 0.0).astype(BF16)
            return jnp.dot(folded_t[...], hot, preferred_element_type=F32)

        def half(values, core):
            return jnp.concatenate(
                [
                    values[start : start + rows_out]
                    for start in range(core * rows_out, MOST, 2 * rows_out)
                ],
                axis=0,
            )

        here = moved(0)
        out[2 * chip] = half(here, 0).astype(BF16)
        if rows % 128 == 0:
            there = half(here, 1)
            out[2 * chip + 1, :, :rows] = there[:, rows:].astype(BF16)
            out[2 * chip + 1, :, rows:] = there[:, :rows].astype(BF16)
        else:
            out[2 * chip + 1] = half(moved(rows), 1).astype(BF16)


def fold_kernel(
    rows, sizes, occ, pair, j_irrep, owner, owner_row, w, out, label_k, blocks, keys, folded
):
    here = lax.axis_index("vir")
    step, part = pl.program_id(0), pl.program_id(1)
    row_block, m_block, columns = w.shape
    wide = out.shape[2]

    @pl.when((step == 0) & (part == 0))
    def _():
        keys[...] = jnp.broadcast_to(column_keys(columns, sizes, j_irrep), keys.shape)

        def clear(s, _):
            blocks[s] = 0
            return 0

        lax.fori_loop(0, blocks.shape[0], clear, 0)

        def visit(k, seen):
            mine = owner[k] == here

            @pl.when(mine)
            def _():
                blocks[seen] = k

            return seen + mine.astype(I32)

        lax.fori_loop(0, owner.shape[0], visit, jnp.int32(0))
        virtuals = owner.shape[0] * BS
        lanes = label_k.shape[1]
        target = coupling_row(owner_row[...], virtuals, rows)
        lane = iota((virtuals, lanes), 1)
        own = here * rows
        mate = (here ^ 1) * rows
        source = jnp.where(lane < rows, lane + own, lane - rows + mate)
        label_e = irrep_of(iota((virtuals, 1), 0), sizes)
        label = jnp.sum(jnp.where(target == source, label_e, 0), axis=0, keepdims=True)
        label_k[...] = jnp.broadcast_to(label, label_k.shape)

    m_row = iota((m_block, 1), 0)
    occ_col = jnp.zeros((m_block, 1), I32)
    for i in range(m_block):
        occ_col = jnp.where(m_row == i, occ[part * m_block + i], occ_col)
    for i in range(row_block):
        row = step * row_block + i
        label = irrep_of(blocks[row // BS] * BS + row % BS, sizes)
        allowed = (occ_col ^ label) == keys[:1, :]
        kept = jnp.where(allowed, w[i].astype(F32), 0.0)
        total = kept[:, :wide]
        for k in range(1, columns // wide):
            total = total + kept[:, k * wide : (k + 1) * wide]
        for k in range(wide // 128):
            folded[k, i * m_block : (i + 1) * m_block, :] = total[:, k * 128 : (k + 1) * 128]
    for i in range(m_block):
        for k in range(wide // 128):
            out[i, :, k * 128 : (k + 1) * 128] = folded[
                k, pl.ds(i, row_block, stride=m_block), :
            ].astype(BF16)


def product_kernel(rows_out, sizes, occ, pair, label_k, t, w_own, w_mate, out):
    step = pl.program_id(0)
    m_block, half, lanes = t.shape
    virtuals = out.shape[0] * 2
    kept_row = iota((out.shape[0], 1), 0)
    core = lax.axis_index("vir") % 2
    a = kept_row // rows_out * (2 * rows_out) + core * rows_out + kept_row % rows_out
    label_a = irrep_of(a, sizes)
    left, right = [], []
    for i in range(m_block):
        wanted = label_k[:1, :] ^ (pair[0] ^ occ[step * m_block + i])
        values = t[i].astype(F32)
        left.append(
            jnp.concatenate(
                [
                    jnp.where(label_a[k : k + half] == wanted, values, 0.0).astype(BF16)
                    for k in range(0, virtuals // 2, half)
                ],
                axis=0,
            )
        )
        right += [w_own[i], w_mate[i]]
    if lanes % 128 == 0:
        total = jnp.dot(
            jnp.concatenate(left, axis=1),
            jnp.concatenate(right, axis=0),
            preferred_element_type=F32,
        )
    else:
        total = jnp.zeros(out.shape, F32)
        for i in range(m_block):
            total = total + jnp.dot(
                left[i],
                jnp.concatenate(right[2 * i : 2 * i + 2], axis=0),
                preferred_element_type=F32,
            )

    @pl.when(step == 0)
    def _():
        out[...] = total

    @pl.when(step > 0)
    def _():
        out[...] += total


def finish_kernel(sizes, pair, j_irrep, parts, out):
    chips, rows_out, wide = parts.shape
    total = parts[0]
    for q in range(1, chips):
        total = total + parts[q]
    columns = out.shape[1]
    a = iota((rows_out, 1), 0) + lax.axis_index("vir") * rows_out
    label_a = irrep_of(a, sizes) ^ pair[0]
    keys = column_keys(columns, sizes, j_irrep)
    for k in range(0, columns, wide):
        out[:, k : k + wide] = jnp.where(label_a == keys[:, k : k + wide], total, 0.0)


def per_device(amplitudes, couplings, occ_irrep, pair_irrep, j_irrep, block_sizes, owner):
    devices = lax.axis_size("vir")
    chips = devices // 2
    virtuals = amplitudes.shape[2]
    rows, occupied, columns = couplings.shape
    wide = columns // virtuals * MOST
    rows_out = virtuals // devices
    lanes = 2 * rows
    blocks = owner.shape[0]
    owner_row = owner.reshape(1, blocks)
    owner_flat = owner.reshape(blocks)
    smem = pl.BlockSpec(memory_space=pltpu.SMEM)
    vmem = pl.BlockSpec(memory_space=pltpu.VMEM)
    params = pltpu.CompilerParams(vmem_limit_bytes=LIMIT)

    chips_step = max(1, 256 // lanes)
    outgoing = pl.pallas_call(
        functools.partial(pack_kernel, rows, rows_out),
        out_shape=jax.ShapeDtypeStruct((devices, MOST // 2, lanes), BF16),
        grid=(chips // chips_step,),
        in_specs=[smem, smem, smem, vmem, pl.BlockSpec(memory_space=pl.ANY)],
        out_specs=pl.BlockSpec((2 * chips_step, MOST // 2, lanes), lambda i: (i, 0, 0)),
        scratch_shapes=[
            pltpu.VMEM((virtuals, virtuals), BF16),
            pltpu.VMEM((MOST, virtuals), BF16),
            pltpu.VMEM((virtuals, 128), I32),
            pltpu.SemaphoreType.DMA,
        ],
        compiler_params=params,
        name="pack_amplitudes",
    )(block_sizes, occ_irrep, pair_irrep, owner_row, amplitudes)
    received = lax.all_to_all(outgoing, "vir", 0, 0)

    row_block, m_block = 16, 16
    w_own, label_k = pl.pallas_call(
        functools.partial(fold_kernel, rows),
        out_shape=(
            jax.ShapeDtypeStruct((occupied, rows, wide), BF16),
            jax.ShapeDtypeStruct((8, lanes), I32),
        ),
        grid=(rows // row_block, occupied // m_block),
        in_specs=[smem, smem, smem, smem, smem, vmem]
        + [pl.BlockSpec((row_block, m_block, columns), lambda i, j: (i, j, 0))],
        out_specs=(
            pl.BlockSpec((m_block, row_block, wide), lambda i, j: (j, i, 0)),
            pl.BlockSpec((8, lanes), lambda i, j: (0, 0)),
        ),
        scratch_shapes=[
            pltpu.SMEM((rows // BS,), I32),
            pltpu.VMEM((8, columns), I32),
            pltpu.VMEM((wide // 128, row_block * m_block, 128), F32),
        ],
        compiler_params=params,
        cost_estimate=pl.CostEstimate(
            flops=4 * rows * occupied * columns,
            bytes_accessed=3 * rows * occupied * columns,
            transcendentals=0,
        ),
        name="fold_couplings",
    )(block_sizes, occ_irrep, pair_irrep, j_irrep, owner_flat, owner_row, couplings)
    w_mate = lax.ppermute(w_own, "vir", [(d, d ^ 1) for d in range(devices)])

    m_step = 4
    kept = virtuals // 2
    partial = pl.pallas_call(
        functools.partial(product_kernel, rows_out),
        out_shape=jax.ShapeDtypeStruct((kept, wide), F32),
        grid=(occupied // m_step,),
        in_specs=[smem, smem, smem, vmem]
        + [pl.BlockSpec((m_step, MOST // 2, lanes), lambda i: (i, 0, 0))]
        + [pl.BlockSpec((m_step, rows, wide), lambda i: (i, 0, 0))] * 2,
        out_specs=pl.BlockSpec((kept, wide), lambda i: (0, 0)),
        compiler_params=params,
        name="multiply",
    )(block_sizes, occ_irrep, pair_irrep, label_k, received, w_own, w_mate)
    sides = [[d for d in range(devices) if d % 2 == core] for core in (0, 1)]
    parts = lax.all_to_all(
        partial.reshape(chips, rows_out, wide), "vir", 0, 0, axis_index_groups=sides
    )
    return pl.pallas_call(
        finish_kernel,
        out_shape=jax.ShapeDtypeStruct((rows_out, columns), F32),
        in_specs=[smem, smem, smem, vmem],
        out_specs=vmem,
        compiler_params=params,
        name="unfold",
    )(block_sizes, pair_irrep, j_irrep, parts)


def solution(mesh):
    return jax.shard_map(
        per_device,
        mesh=mesh,
        in_specs=(
            P(("grp", "vir"), None, None),
            P(("grp", "vir"), None, None),
            P("grp"),
            P(),
            P(),
            P("grp"),
            P("grp", None),
        ),
        out_specs=P(("grp", "vir"), None),
        check_vma=False,
    )
```

time: 344 us -> 92.1 us (0.27)
  waiting for transfers between devices: 188 us -> 0.01 us
  local copies, waits for them, and re-layouts: 71.6 us -> 3.99 us
  blocking collectives: 0 us -> 62.6 us
  other arithmetic: 42.1 us -> 0 us
  Pallas kernels: 0 us -> 24 us
  matrix products: 19 us -> 0 us
  between operations: 14.8 us -> 0.7 us
  starting transfers between devices: 7.79 us -> 0.52 us
    reduce_scatter x1 -> x0, waiting for transfers between devices: 120 us -> none  [per_device(): lax.psum_scatter(lax.dot_general(received, masked_w, (((0, 1), (1, 0)), (...]
    all_to_all x1 -> x0, waiting for transfers between devices: 67.9 us -> none  [per_device(): lax.all_to_all(outgoing, 'vir', split_axis=1, concat_axis=0, tiled=True)]
    all_to_all x0 -> x2, blocking collectives: none -> 62.6 us  [the longest x1 31.7 us: per_device(): received = lax.all_to_all(outgoing, 'vir', 0, 0)]
    select_n x1 -> x0, local copies, waits for them, and re-layouts: 28.7 us -> none  [per_device(): jnp.where(e_filled[None, :, None], outgoing, jnp.zeros((), outgoing.dtype))]
    unnamed x10 -> x14, local copies, waits for them, and re-layouts: 30.1 us -> 3.99 us
    unnamed x1 -> x0, other arithmetic: 26 us -> none
    pallas_call x0 -> x4, Pallas kernels: none -> 24 us  [the longest x1 11.9 us: per_device(): pl.pallas_call(functools.partial(fold_kernel, rows), out_shape=(jax.Shape...]
    dot_general x1 -> x0, matrix products: 19 us -> none  [per_device(): lax.dot_general(received, masked_w, (((0, 1), (1, 0)), ((), ())), preferr...]
  transfers between devices with their start and end apart: 2 -> 1, of which waited for: 2 -> 0; matrix products, arithmetic and copies ran while one was open for 3% -> 0% of each run, Pallas kernels for 0% -> 6%
where the time goes in v1:
time: 92.1 us; the launch traced here: 91.7 us
  blocking collectives  62.6 us (68%)
  Pallas kernels  24 us (26%)
  local copies, waits for them, and re-layouts  3.99 us (4%)
    all_to_all x1, blocking collectives, per_device(): received = lax.all_to_all(outgoing, 'vir', 0, 0)  31.7 us
    all_to_all x1, blocking collectives, per_device(): lax.all_to_all(partial.reshape(chips, rows_out, wide), 'vir', 0, 0, axis_...  30.9 us
    pallas_call x1, Pallas kernels, per_device(): pl.pallas_call(functools.partial(fold_kernel, rows), out_shape=(jax.Shape...  11.9 us
    pallas_call x1, Pallas kernels, per_device(): pl.pallas_call(functools.partial(pack_kernel, rows, rows_out), out_shape=...  5.63 us
    pallas_call x1, Pallas kernels, per_device(): pl.pallas_call(functools.partial(product_kernel, rows_out), out_shape=jax...  4.91 us
    unnamed x14, local copies, waits for them, and re-layouts  3.99 us
  transfers between devices with their start and end apart: 1, of which 0 were waited for; matrix products, arithmetic and copies ran while one was open for 0% of the time, Pallas kernels for 6%

profile of v1, /device:TPU:0, one launch (start us, length us, event | category | flops | bytes accessed | tf_op | source)
XLA Modules:
  0.0 91.7 jit_solution(5275543843796568781)
XLA Ops:
  0.7 0.0 copy-start.1
  0.7 0.7 copy-done.1
  1.3 0.0 copy-start.2
  1.3 0.7 copy-done.2
  2.0 0.0 copy-start.3
  2.0 0.7 copy-done.3
  2.6 0.0 copy-start.4
  2.6 0.7 copy-done.4
  3.3 0.0 copy-start
  3.3 11.9 %fold_couplings.1 = (bf16[16,128,512]{2,1,0:T(8,128)(2,1)S(1)}, s32[8,256]{1,0:T(8,128)S(1)}) custom-call(s32[8]{0:T(128)S(1)} %copy-done.2, s32[16]{0:T(128)S(1)} %copy-done.3, s32[1]{0:T(128)S(6)} %copy.8.pair, s32[2]{0:T(128)S(1)} %copy-done.4, s32[256]{0:T(256)S(1)} %bitcast.4, s32[1,256]{1,0:T(1,128)S(1)} %bitcast.5, bf16[128,16,2048]{2,1,0:T(8,128)(2,1)} %w.1), custom_call_target="tpu_custom_call" | custom-call | flops 16777216 | bytes 12582912 | tf_op jit(solution)/shard_map/fold_couplings/pallas_call | solution.py:258
  15.2 0.5 collective-permute-start
  15.7 0.0 copy-done
  15.7 5.6 %pack_amplitudes.1 = bf16[16,128,256]{2,1,0:T(8,128)(2,1)S(1)} custom-call(s32[8]{0:T(128)S(1)} %copy-done.2, s32[16]{0:T(128)S(1)} %copy-done.3, s32[1]{0:T(128)S(6)} %copy.8.pair, s32[1,256]{1,0:T(1,128)S(1)} %bitcast.6, bf16[1,1024,1024]{2,1,0:T(8,128)(2,1)S(1)} %copy-done), custom_call_target="tpu_custom_call" | custom-call | tf_op jit(solution)/shard_map/pack_amplitudes/pallas_call | solution.py:240
  21.4 31.7 %all_to_all.10.t = bf16[16,128,256]{2,1,0:T(8,128)(2,1)S(1)} all-to-all(bf16[16,128,256]{2,1,0:T(8,128)(2,1)S(1)} %pack_amplitudes.1), channel_id=1, replica_groups=mesh['grp'=2,'vir'=16] {'vir'}, dimensions={0} | all-to-all | bytes 2097152 | tf_op jit(solution)/shard_map/all_to_all | solution.py:255
  53.1 0.0 collective-permute-done.w_mate
  53.1 0.0 copy-start.6
  53.1 1.3 %copy-done.6 = bf16[16,128,512]{2,1,0:T(8,128)(2,1)} copy-done((bf16[16,128,512]{2,1,0:T(8,128)(2,1)}, bf16[16,128,512]{2,1,0:T(8,128)(2,1)S(1)}, u32[]{:S(2)}) %copy-start.6) | copy-done | bytes 2097176
  54.4 4.9 %multiply.1 = f32[512,512]{1,0:T(8,128)S(1)} custom-call(s32[8]{0:T(128)S(1)} %copy-done.2, s32[16]{0:T(128)S(1)} %copy-done.3, s32[1]{0:T(128)S(6)} %copy.8.pair, s32[8,256]{1,0:T(8,128)S(1)} %get-tuple-element.7.label_k, bf16[16,128,256]{2,1,0:T(8,128)(2,1)S(1)} %all_to_all.10.t, bf16[16,128,512]{2,1,0:T(8,128)(2,1)S(1)} %get-tuple-element.8.w_own, ...), custom_call_target="tpu_custom_call" | custom-call | tf_op jit(solution)/shard_map/multiply/pallas_call | solution.py:288
  59.4 0.0 copy-start.5
  59.4 30.9 %all_to_all.11.parts = f32[8,64,512]{2,1,0:T(8,128)S(1)} all-to-all(f32[8,64,512]{2,1,0:T(8,128)S(1)} %bitcast.3), channel_id=1, replica_groups={{0,2,4,6,8,10,12,14},{1,3,5,7,9,11,13,15},{16,18,20,22,24,26,28,30},{17..., dimensions={0} | all-to-all | bytes 2097152 | tf_op jit(solution)/shard_map/all_to_all | solution.py:300
  90.2 0.0 copy-done.5
  90.2 1.5 %unfold.1 = f32[64,2048]{1,0:T(8,128)} custom-call(s32[8]{0:T(128)S(1)} %copy-done.2, s32[1]{0:T(128)S(6)} %copy.8.pair, s32[2]{0:T(128)S(1)} %copy-done.5, f32[8,64,512]{2,1,0:T(8,128)S(1)} %all_to_all.11.parts), custom_call_target="tpu_custom_call" | custom-call | tf_op jit(solution)/shard_map/unfold/pallas_call | solution.py:303
Async XLA Ops:
  0.7 0.7 copy-start.1
  1.3 0.7 copy-start.2
  2.0 0.7 copy-start.3
  2.6 0.7 copy-start.4
  3.3 12.4 %copy-start = (bf16[1,1024,1024]{2,1,0:T(8,128)(2,1)S(1)}, bf16[1,1024,1024]{2,1,0:T(8,128)(2,1)}, u32[]{:S(2)}) copy-start(bf16[1,1024,1024]{2,1,0:T(8,128)(2,1)} %t_hbm.1) | copy-start | bytes 6291460
  15.2 37.9 %collective-permute-start = (bf16[16,128,512]{2,1,0:T(8,128)(2,1)S(1)}, bf16[16,128,512]{2,1,0:T(8,128)(2,1)S(1)}, u32[]{:S(2)}, u32[]{:S(2)}) collective-permute-start(bf16[16,128,512]{2,1,0:T(8,128)(2,1)S(1)} %get-tuple-element.8.w_own), channel_id=1, source_target_pairs={{0,1},{1,0},{2,3},{3,2},{4,5},{5,4},{6,7},{7,6},{8,9},{9,8},{10,11... | collective-permute-start | bytes 6291464 | tf_op jit(solution)/shard_map/ppermute | solution.py:284
  53.1 1.3 %copy-start.6 = (bf16[16,128,512]{2,1,0:T(8,128)(2,1)}, bf16[16,128,512]{2,1,0:T(8,128)(2,1)S(1)}, u32[]{:S(2)}) copy-start(bf16[16,128,512]{2,1,0:T(8,128)(2,1)S(1)} %collective-permute-done.w_mate) | copy-start | bytes 6291460
  59.4 30.9 %copy-start.5 = (s32[2]{0:T(128)S(1)}, s32[2]{0:T(128)}, u32[]{:S(2)}) copy-start(s32[2]{0:T(128)} %j_irrep.3) | copy-start | bytes 28

commit v2 on v1

v2 whole, which is shorter than its diff:
```python
import functools

import jax
import jax.numpy as jnp
from jax import lax
from jax.experimental import pallas as pl
from jax.experimental.pallas import tpu as pltpu
from jax.sharding import PartitionSpec as P

BS = 4
MOST = 256
LIMIT = 24 * 1024 * 1024
MOST_LIMIT = 60 * 1024 * 1024
F32, BF16, I32 = jnp.float32, jnp.bfloat16, jnp.int32


def irrep_of(index, sizes):
    label = jnp.zeros_like(index)
    end = jnp.int32(0)
    for h in range(sizes.shape[0]):
        end = end + sizes[h]
        label = label + (index >= end).astype(I32)
    return label


def iota(shape, dim):
    return lax.broadcasted_iota(I32, shape, dim)


def column_keys(columns, sizes, j_irrep):
    count = j_irrep.shape[0]
    column = iota((1, columns), 1)
    j = column % count
    j_label = jnp.zeros_like(column)
    for i in range(count):
        j_label = jnp.where(j == i, j_irrep[i], j_label)
    return irrep_of(column // count, sizes) ^ j_label


def block_place(owner_row, rows):
    blocks = owner_row.shape[1]
    first, second = iota((blocks, blocks), 0), iota((blocks, blocks), 1)
    owner_col = jnp.sum(jnp.where(first == second, owner_row, 0), axis=1, keepdims=True)
    earlier = (owner_col == owner_row) & (first < second)
    rank = jnp.sum(earlier.astype(I32), axis=0, keepdims=True)
    return owner_row * rows + rank * BS


def virtual_place(place, virtuals):
    blocks = place.shape[1]
    e, block = iota((virtuals, blocks), 0), iota((virtuals, blocks), 1)
    start = jnp.sum(jnp.where(e // BS == block, place, 0), axis=1, keepdims=True)
    return start + iota((virtuals, 1), 0) % BS


def pack_kernel(
    rows,
    rows_out,
    sizes_hbm,
    occ_hbm,
    pair_hbm,
    owner_hbm,
    t_hbm,
    out,
    place,
    sizes,
    occ,
    pair,
    owner_row,
    t_vmem,
    folded_t,
    target,
    sems,
):
    virtuals = t_hbm.shape[1]
    lanes = 2 * rows

    @pl.when(pl.program_id(0) == 0)
    def _():
        pairs = (
            (owner_hbm, owner_row),
            (sizes_hbm, sizes),
            (occ_hbm, occ),
            (pair_hbm, pair),
            (t_hbm.at[0], t_vmem),
        )
        copies = [
            pltpu.make_async_copy(source, here, sems.at[i])
            for i, (source, here) in enumerate(pairs)
        ]
        for copy in copies:
            copy.start()
        copies[0].wait()
        where = block_place(owner_row[...], rows)
        place[...] = jnp.broadcast_to(where, place.shape)
        target[...] = jnp.broadcast_to(virtual_place(where, virtuals), target.shape)
        for copy in copies[1:4]:
            copy.wait()
        wanted = pair[0] ^ occ[lax.axis_index("vir")]
        label_e = irrep_of(iota((virtuals, 1), 0), sizes) ^ wanted
        label_a = irrep_of(iota((1, virtuals), 1), sizes)
        copies[4].wait()
        folded = jnp.zeros((virtuals, MOST), F32)
        for k in range(virtuals // MOST):
            part = slice(k * MOST, (k + 1) * MOST)
            folded = folded + jnp.where(
                label_e == label_a[:, part], t_vmem[:, part].astype(F32), 0.0
            )
        folded_t[...] = folded.T.astype(BF16)

    chips = out.shape[0] // 2
    for chip in range(chips):
        lane = iota((virtuals, lanes), 1)
        offset = (pl.program_id(0) * chips + chip) * lanes
        place = target[:, :1] - offset

        def moved(flip):
            hot = jnp.where(place == lane ^ flip, 1.0, 0.0).astype(BF16)
            return jnp.dot(folded_t[...], hot, preferred_element_type=F32)

        def half(values, core):
            return jnp.concatenate(
                [
                    values[start : start + rows_out]
                    for start in range(core * rows_out, MOST, 2 * rows_out)
                ],
                axis=0,
            )

        here = moved(0)
        out[2 * chip] = half(here, 0).astype(BF16)
        if rows % 128 == 0:
            there = half(here, 1)
            out[2 * chip + 1, :, :rows] = there[:, rows:].astype(BF16)
            out[2 * chip + 1, :, rows:] = there[:, :rows].astype(BF16)
        else:
            out[2 * chip + 1] = half(moved(rows), 1).astype(BF16)


def label_kernel(
    rows,
    rows_out,
    sizes,
    occ,
    pair,
    j_irrep,
    place,
    label_row,
    label_k,
    label_kept,
    label_out,
    keys,
):
    here = lax.axis_index("vir")
    occupied, lanes = label_k.shape
    virtuals = place.shape[1] * BS
    target = virtual_place(place[:1, :], virtuals)
    lane = iota((virtuals, lanes), 1)
    source = jnp.where(lane < rows, lane + here * rows, lane - rows + (here ^ 1) * rows)
    label_e = irrep_of(iota((virtuals, 1), 0), sizes)
    label = jnp.sum(jnp.where(target == source, label_e, 0), axis=0, keepdims=True)
    label_row[...] = label[:, :rows]
    for m in range(occupied):
        label_k[m : m + 1, :] = label ^ (pair[0] ^ occ[m])
    row = iota(label_kept.shape, 0)
    a = row // rows_out * (2 * rows_out) + here % 2 * rows_out + row % rows_out
    label_kept[...] = irrep_of(a, sizes)
    label_out[...] = irrep_of(iota(label_out.shape, 0) + here * rows_out, sizes) ^ pair[0]
    keys[...] = jnp.broadcast_to(column_keys(keys.shape[1], sizes, j_irrep), keys.shape)


def fold_kernel(first, occ, label_row, keys, w, out, folded):
    step, part = pl.program_id(0), pl.program_id(1)
    row_block, m_block, columns = w.shape
    wide = out.shape[2]
    m_row = iota((m_block, 1), 0)
    occ_col = jnp.zeros((m_block, 1), I32)
    for i in range(m_block):
        occ_col = jnp.where(m_row == i, occ[part * m_block + i], occ_col)
    for i in range(row_block):
        label = label_row[first + step * row_block + i]
        allowed = (occ_col ^ label) == keys[:1, :]
        kept = jnp.where(allowed, w[i].astype(F32), 0.0)
        total = kept[:, :wide]
        for k in range(1, columns // wide):
            total = total + kept[:, k * wide : (k + 1) * wide]
        for k in range(wide // 128):
            folded[k, i * m_block : (i + 1) * m_block, :] = total[:, k * 128 : (k + 1) * 128]
    for i in range(m_block):
        for k in range(wide // 128):
            out[i, :, k * 128 : (k + 1) * 128] = folded[
                k, pl.ds(i, row_block, stride=m_block), :
            ].astype(BF16)


def product_kernel(label_k_hbm, label_kept_hbm, t_hbm, *refs):
    *pieces, out, label_k, label_kept, t, w, sems = refs
    occupied, half, lanes = t.shape
    kept = out.shape[0]
    size = pieces[0].shape[1]
    m_block = max(1, min(occupied, 1024 // lanes))
    steps = occupied // m_block

    def fetches(step):
        part = pl.ds(step * m_block, m_block)
        pairs = [(t_hbm.at[part], t.at[part])] + [
            (piece.at[part], w.at[part, pl.ds(i * size, size)])
            for i, piece in enumerate(pieces)
        ]
        return [
            pltpu.make_async_copy(source, here, sems.at[2 + step * len(pairs) + i])
            for i, (source, here) in enumerate(pairs)
        ]

    tables = [
        pltpu.make_async_copy(label_k_hbm, label_k, sems.at[0]),
        pltpu.make_async_copy(label_kept_hbm, label_kept, sems.at[1]),
    ]
    for copy in tables:
        copy.start()
    for step in range(steps):
        for copy in fetches(step):
            copy.start()
    out[...] = jnp.zeros(out.shape, F32)
    for copy in tables:
        copy.wait()
    wide_label = jnp.broadcast_to(label_kept[:, :1], (kept, lanes))

    @pl.loop(0, steps)
    def _(step):
        for copy in fetches(step):
            copy.wait()
        left, right = [], []
        for i in range(m_block):
            m = step * m_block + i
            wanted = label_k[pl.ds(m, 1), :]
            values = t[m].astype(F32)
            left.append(
                jnp.concatenate(
                    [
                        jnp.where(wide_label[k : k + half] == wanted, values, 0.0).astype(BF16)
                        for k in range(0, kept, half)
                    ],
                    axis=0,
                )
            )
            right.append(w[m])
        if lanes % 128 == 0:
            left = [jnp.concatenate(left, axis=1)]
            right = [jnp.concatenate(right, axis=0)]
        total = jnp.dot(left[0], right[0], preferred_element_type=F32)
        for x, y in zip(left[1:], right[1:]):
            total = total + jnp.dot(x, y, preferred_element_type=F32)
        out[...] += total


def finish_kernel(label_out, keys, parts, out):
    chips, rows_out, wide = parts.shape
    total = parts[0]
    for q in range(1, chips):
        total = total + parts[q]
    for k in range(0, out.shape[1], wide):
        out[:, k : k + wide] = jnp.where(
            label_out[:, :1] == keys[:1, k : k + wide], total, 0.0
        )


def per_device(amplitudes, couplings, occ_irrep, pair_irrep, j_irrep, block_sizes, owner):
    devices = lax.axis_size("vir")
    chips = devices // 2
    virtuals = amplitudes.shape[2]
    rows, occupied, columns = couplings.shape
    wide = columns // virtuals * MOST
    rows_out = virtuals // devices
    kept = virtuals // 2
    lanes = 2 * rows
    blocks = owner.shape[0]
    smem = pl.BlockSpec(memory_space=pltpu.SMEM)
    vmem = pl.BlockSpec(memory_space=pltpu.VMEM)
    hbm = pl.BlockSpec(memory_space=pltpu.HBM)
    params = pltpu.CompilerParams(vmem_limit_bytes=LIMIT)
    alone = pltpu.CompilerParams(vmem_limit_bytes=MOST_LIMIT)

    chips_step = max(1, 256 // lanes)
    outgoing, place = pl.pallas_call(
        functools.partial(pack_kernel, rows, rows_out),
        out_shape=(
            jax.ShapeDtypeStruct((devices, MOST // 2, lanes), BF16),
            jax.ShapeDtypeStruct((8, blocks), I32),
        ),
        grid=(chips // chips_step,),
        in_specs=[hbm] * 5,
        out_specs=(
            pl.BlockSpec((2 * chips_step, MOST // 2, lanes), lambda i: (i, 0, 0)),
            pl.BlockSpec((8, blocks), lambda i: (0, 0)),
        ),
        scratch_shapes=[
            pltpu.SMEM(block_sizes.shape, I32),
            pltpu.SMEM(occ_irrep.shape, I32),
            pltpu.SMEM(pair_irrep.shape, I32),
            pltpu.VMEM((1, blocks), I32),
            pltpu.VMEM((virtuals, virtuals), BF16),
            pltpu.VMEM((MOST, virtuals), BF16),
            pltpu.VMEM((virtuals, 128), I32),
            pltpu.SemaphoreType.DMA((5,)),
        ],
        compiler_params=alone,
        name="pack_amplitudes",
    )(block_sizes, occ_irrep, pair_irrep, owner.reshape(1, blocks), amplitudes)
    received = lax.all_to_all(outgoing, "vir", 0, 0)

    label_row, label_k, label_kept, label_out, keys = pl.pallas_call(
        functools.partial(label_kernel, rows, rows_out),
        out_shape=(
            jax.ShapeDtypeStruct((1, rows), I32),
            jax.ShapeDtypeStruct((occupied, lanes), I32),
            jax.ShapeDtypeStruct((kept, 128), I32),
            jax.ShapeDtypeStruct((rows_out, 128), I32),
            jax.ShapeDtypeStruct((8, columns), I32),
        ),
        in_specs=[smem] * 4 + [vmem],
        out_specs=(vmem,) * 5,
        compiler_params=params,
        name="labels",
    )(block_sizes, occ_irrep, pair_irrep, j_irrep, place)

    row_block, m_block = 16, 16
    pieces = max(1, rows // 32)
    piece_rows = rows // pieces
    w_own, w_mate = [], []
    for piece in range(pieces):
        first = piece * piece_rows
        w_own.append(
            pl.pallas_call(
                functools.partial(fold_kernel, first),
                out_shape=jax.ShapeDtypeStruct((occupied, piece_rows, wide), BF16),
                grid=(piece_rows // row_block, occupied // m_block),
                in_specs=[smem, smem, vmem]
                + [
                    pl.BlockSpec(
                        (row_block, m_block, columns),
                        lambda i, j, skip=first // row_block: (skip + i, j, 0),
                    )
                ],
                out_specs=pl.BlockSpec((m_block, row_block, wide), lambda i, j: (j, i, 0)),
                scratch_shapes=[pltpu.VMEM((wide // 128, row_block * m_block, 128), F32)],
                compiler_params=params,
                cost_estimate=pl.CostEstimate(
                    flops=4 * piece_rows * occupied * columns,
                    bytes_accessed=3 * piece_rows * occupied * columns,
                    transcendentals=0,
                ),
                name="fold_couplings",
            )(occ_irrep, label_row.reshape(rows), keys, couplings)
        )
        w_mate.append(lax.ppermute(w_own[-1], "vir", [(d, d ^ 1) for d in range(devices)]))

    partial = pl.pallas_call(
        product_kernel,
        out_shape=jax.ShapeDtypeStruct((kept, wide), F32),
        in_specs=[hbm] * (3 + 2 * pieces),
        out_specs=vmem,
        scratch_shapes=[
            pltpu.VMEM((occupied, lanes), I32),
            pltpu.VMEM((kept, 128), I32),
            pltpu.VMEM(received.shape, BF16),
            pltpu.VMEM((occupied, lanes, wide), BF16),
            pltpu.SemaphoreType.DMA((2 + occupied * (1 + 2 * pieces),)),
        ],
        compiler_params=alone,
        name="multiply",
    )(label_k, label_kept, received, *w_own, *w_mate)
    sides = [[d for d in range(devices) if d % 2 == core] for core in (0, 1)]
    parts = lax.all_to_all(
        partial.reshape(chips, rows_out, wide), "vir", 0, 0, axis_index_groups=sides
    )
    return pl.pallas_call(
        finish_kernel,
        out_shape=jax.ShapeDtypeStruct((rows_out, columns), F32),
        in_specs=[vmem] * 3,
        out_specs=vmem,
        compiler_params=params,
        name="unfold",
    )(label_out, keys, parts)


def solution(mesh):
    return jax.shard_map(
        per_device,
        mesh=mesh,
        in_specs=(
            P(("grp", "vir"), None, None),
            P(("grp", "vir"), None, None),
            P("grp"),
            P(),
            P(),
            P("grp"),
            P("grp", None),
        ),
        out_specs=P(("grp", "vir"), None),
        check_vma=False,
    )
```

time: 92.1 us -> 80.5 us (0.87)
  blocking collectives: 62.6 us -> 33 us
  starting transfers between devices: 0.52 us -> 8.69 us
  waiting for transfers between devices: 0.01 us -> 5.3 us
  local copies, waits for them, and re-layouts: 3.99 us -> 9.24 us
    all_to_all x1 -> x0, blocking collectives: 31.7 us -> none  [per_device(): received = lax.all_to_all(outgoing, 'vir', 0, 0)]
    all_to_all x0 -> x1, starting transfers between devices: none -> 7.4 us  [per_device(): received = lax.all_to_all(outgoing, 'vir', 0, 0)]
    unnamed x14 -> x32, local copies, waits for them, and re-layouts: 3.99 us -> 9.24 us
    all_to_all x0 -> x1, waiting for transfers between devices: none -> 4.24 us  [per_device(): received = lax.all_to_all(outgoing, 'vir', 0, 0)]
    pallas_call x2 -> x6, Pallas kernels: 16.8 us -> 14.6 us  [the longest x1 6.65 us: per_device(): pl.pallas_call(product_kernel, out_shape=jax.ShapeDtypeStruct((kept, wide...]
    all_to_all x1, blocking collectives: 30.9 us -> 33 us  [per_device(): lax.all_to_all(partial.reshape(chips, rows_out, wide), 'vir', 0, 0, axis_...]
    pallas_call x1, Pallas kernels: 5.63 us -> 7.61 us  [per_device(): pl.pallas_call(functools.partial(pack_kernel, rows, rows_out), out_shape=...]
    ppermute x1 -> x4, waiting for transfers between devices: 0.01 us -> 1.06 us  [per_device(): lax.ppermute(w_own[-1], 'vir', [(d, d ^ 1) for d in range(devices)])]
  transfers between devices with their start and end apart: 1 -> 5, of which waited for: 0 -> 2; matrix products, arithmetic and copies ran while one was open for 0% -> 0% of each run, Pallas kernels for 6% -> 10%
where the time goes in v2:
time: 80.5 us; the launch traced here: 80.1 us
  blocking collectives  33 us (41%)
  Pallas kernels  23.1 us (29%)
  local copies, waits for them, and re-layouts  9.24 us (11%)
  starting transfers between devices  8.69 us (11%)
  waiting for transfers between devices  5.3 us (7%)
  between operations  0.84 us (1%)
    all_to_all x1, blocking collectives, per_device(): lax.all_to_all(partial.reshape(chips, rows_out, wide), 'vir', 0, 0, axis_...  33 us
    unnamed x32, local copies, waits for them, and re-layouts  9.24 us
    pallas_call x1, Pallas kernels, per_device(): pl.pallas_call(functools.partial(pack_kernel, rows, rows_out), out_shape=...  7.61 us
    all_to_all x1, starting transfers between devices, per_device(): received = lax.all_to_all(outgoing, 'vir', 0, 0)  7.4 us
    pallas_call x1, Pallas kernels, per_device(): pl.pallas_call(product_kernel, out_shape=jax.ShapeDtypeStruct((kept, wide...  6.65 us
    pallas_call x4, Pallas kernels, per_device(): pl.pallas_call(functools.partial(fold_kernel, first), out_shape=jax.Shape...  6.12 us
    all_to_all x1, waiting for transfers between devices, per_device(): received = lax.all_to_all(outgoing, 'vir', 0, 0)  4.24 us
    pallas_call x1, Pallas kernels, per_device(): pl.pallas_call(functools.partial(label_kernel, rows, rows_out), out_shape...  1.84 us
  transfers between devices with their start and end apart: 5, of which 2 were waited for; matrix products, arithmetic and copies ran while one was open for 0% of the time, Pallas kernels for 10%

profile of v2, /device:TPU:0, one launch (start us, length us, event | category | flops | bytes accessed | tf_op | source)
XLA Modules:
  0.0 80.1 jit_solution(17693325282548474848)
XLA Ops:
  0.7 7.6 %pack_amplitudes.1 = (bf16[16,128,256]{2,1,0:T(8,128)(2,1)}, s32[8,256]{1,0:T(8,128)}) custom-call(s32[8]{0:T(128)} %sizes.1, s32[16]{0:T(128)} %occ.9, s32[1]{0:T(128)S(6)} %copy.8.pair_hbm.pair, s32[1,256]{1,0:T(1,128)} %bitcast.8, bf16[1,1024,1024]{2,1,0:T(8,128)(2,1)} %t_hbm.1), custom_call_target="tpu_custom_call" | custom-call | tf_op jit(solution)/shard_map/pack_amplitudes/pallas_call | solution.py:285
  8.3 7.4 %all-to-all-start = ((bf16[16,128,256]{2,1,0:T(8,128)(2,1)}), bf16[16,128,256]{2,1,0:T(8,128)(2,1)S(1)}, u32[]{:S(2)}, u32[]{:S(2)}) async-start(bf16[16,128,256]{2,1,0:T(8,128)(2,1)} %get-tuple-element.17), calls=%async_computation | async-start | bytes 2097152 | tf_op jit(solution)/shard_map/all_to_all | solution.py:310
  15.7 0.0 copy-start.6
  15.7 0.6 copy-done.6
  16.3 0.0 copy-start.9
  16.3 0.7 copy-done.9
  17.0 0.0 copy-start.10
  17.0 0.7 copy-done.10
  17.7 0.0 copy-start.11
  17.7 0.7 copy-done.11
  18.4 1.8 %labels.1 = (s32[1,128]{1,0:T(1,128)S(1)}, s32[16,256]{1,0:T(8,128)S(1)}, s32[512,128]{1,0:T(8,128)S(1)}, s32[64,128]{1,0:T(8,128)S(1)}, s32[8,2048]{1,0:T(8,128)S(1)}) custom-call(s32[8]{0:T(128)S(1)} %copy-done.10, s32[16]{0:T(128)S(1)} %copy-done.6, s32[1]{0:T(128)S(6)} %copy.8.pair_hbm.pair, s32[2]{0:T(128)S(1)} %copy-done.11, s32[8,256]{1,0:T(8,128)S(1)} %copy-done.9), custom_call_target="tpu_custom_call" | custom-call | tf_op jit(solution)/shard_map/labels/pallas_call | solution.py:312
  20.2 0.0 copy-start.5
  20.2 0.7 copy-done.5
  20.9 0.0 copy-start.8
  20.9 0.0 copy-start
  20.9 3.4 %copy-done = bf16[128,16,2048]{2,1,0:T(8,128)(2,1)S(1)} copy-done((bf16[128,16,2048]{2,1,0:T(8,128)(2,1)S(1)}, bf16[128,16,2048]{2,1,0:T(8,128)(2,1)}, u32[]{:S(2)}) %copy-start) | copy-done | bytes 8388632
  24.3 0.7 copy-done.7
  24.9 1.5 %fold_couplings.4.refs_0_ = bf16[16,32,512]{2,1,0:T(8,128)(2,1)S(1)} custom-call(s32[16]{0:T(128)S(1)} %copy-done.7, s32[128]{0:T(128)S(1)} %bitcast.3, s32[8,2048]{1,0:T(8,128)S(1)} %get-tuple-element.14.keys, bf16[128,16,2048]{2,1,0:T(8,128)(2,1)S(1)} %copy-done), custom_call_target="tpu_custom_call" | custom-call | flops 4194304 | bytes 3145728 | tf_op jit(solution)/shard_map/fold_couplings/pallas_call | solution.py:334
  26.5 0.0 copy-start.1
  26.5 0.5 collective-permute-start
  27.0 1.5 %fold_couplings.5.refs_1_ = bf16[16,32,512]{2,1,0:T(8,128)(2,1)S(1)} custom-call(s32[16]{0:T(128)S(1)} %copy-done.7, s32[128]{0:T(128)S(1)} %bitcast.4, s32[8,2048]{1,0:T(8,128)S(1)} %get-tuple-element.14.keys, bf16[128,16,2048]{2,1,0:T(8,128)(2,1)S(1)} %copy-done), custom_call_target="tpu_custom_call" | custom-call | flops 4194304 | bytes 3145728 | tf_op jit(solution)/shard_map/fold_couplings/pallas_call | solution.py:334
  28.5 0.0 copy-done.8
  28.5 0.0 copy-start.2
  28.5 0.2 collective-permute-start.1
  28.7 1.5 %fold_couplings.6.refs_2_ = bf16[16,32,512]{2,1,0:T(8,128)(2,1)S(1)} custom-call(s32[16]{0:T(128)S(1)} %copy-done.7, s32[128]{0:T(128)S(1)} %bitcast.5, s32[8,2048]{1,0:T(8,128)S(1)} %get-tuple-element.14.keys, bf16[128,16,2048]{2,1,0:T(8,128)(2,1)S(1)} %copy-done), custom_call_target="tpu_custom_call" | custom-call | flops 4194304 | bytes 3145728 | tf_op jit(solution)/shard_map/fold_couplings/pallas_call | solution.py:334
  30.2 0.0 copy-done.1
  30.2 0.0 copy-start.3
  30.2 0.5 collective-permute-start.2
  30.7 1.5 %fold_couplings.7.refs_3_ = bf16[16,32,512]{2,1,0:T(8,128)(2,1)S(1)} custom-call(s32[16]{0:T(128)S(1)} %copy-done.7, s32[128]{0:T(128)S(1)} %bitcast.6, s32[8,2048]{1,0:T(8,128)S(1)} %get-tuple-element.14.keys, bf16[128,16,2048]{2,1,0:T(8,128)(2,1)S(1)} %copy-done), custom_call_target="tpu_custom_call" | custom-call | flops 4194304 | bytes 3145728 | tf_op jit(solution)/shard_map/fold_couplings/pallas_call | solution.py:334
  32.3 0.0 copy-done.2
  32.3 0.0 copy-start.4
  32.3 0.2 collective-permute-start.3
  32.4 0.0 collective-permute-done.refs_4_
  32.5 0.0 collective-permute-done.1.refs_5_
  32.5 0.0 copy-start.14
  32.5 0.0 collective-permute-done.2.refs_6_
  32.5 0.0 copy-start.15
  32.5 0.8 %copy-done.15 = bf16[16,32,512]{2,1,0:T(8,128)(2,1)} copy-done((bf16[16,32,512]{2,1,0:T(8,128)(2,1)}, bf16[16,32,512]{2,1,0:T(8,128)(2,1)S(1)}, u32[]{:S(2)}) %copy-start.15) | copy-done | bytes 524312
  33.3 1.0 %collective-permute-done.3.refs_7_ = bf16[16,32,512]{2,1,0:T(8,128)(2,1)} collective-permute-done((bf16[16,32,512]{2,1,0:T(8,128)(2,1)S(1)}, bf16[16,32,512]{2,1,0:T(8,128)(2,1)}, u32[]{:S(2)}, u32[]{:S(2)}) %collective-permute-start.3) | collective-permute-done | bytes 524320 | tf_op jit(solution)/shard_map/ppermute | solution.py:356
  34.4 4.2 %all-to-all-done.t_hbm = bf16[16,128,256]{2,1,0:T(8,128)(2,1)S(1)} async-done(((bf16[16,128,256]{2,1,0:T(8,128)(2,1)}), bf16[16,128,256]{2,1,0:T(8,128)(2,1)S(1)}, u32[]{:S(2)}, u32[]{:S(2)}) %all-to-all-start) | async-done | bytes 1048608 | tf_op jit(solution)/shard_map/all_to_all | solution.py:310
  38.6 0.0 copy-done.3
  38.6 0.0 copy-done.4
  38.6 0.0 copy-done.13
  38.6 0.0 copy-done.14
  38.6 1.0 %copy-done.12 = bf16[16,128,256]{2,1,0:T(8,128)(2,1)} copy-done((bf16[16,128,256]{2,1,0:T(8,128)(2,1)}, bf16[16,128,256]{2,1,0:T(8,128)(2,1)S(1)}, u32[]{:S(2)}) %copy-start.12) | copy-done | bytes 1048600
  39.6 6.7 %multiply.1 = f32[512,512]{1,0:T(8,128)} custom-call(s32[16,256]{1,0:T(8,128)} %copy-done.8, s32[512,128]{1,0:T(8,128)} %copy-done.5, bf16[16,128,256]{2,1,0:T(8,128)(2,1)} %copy-done.12, bf16[16,32,512]{2,1,0:T(8,128)(2,1)} %copy-done.1, bf16[16,32,512]{2,1,0:T(8,128)(2,1)} %copy-done.2, bf16[16,32,512]{2,1,0:T(8,128)(2,1)} %copy-done.3, ...), custom_call_target="tpu_custom_call" | custom-call | tf_op jit(solution)/shard_map/multiply/pallas_call | solution.py:358
  46.3 33.0 %all_to_all.10.parts = f32[8,64,512]{2,1,0:T(8,128)S(1)} all-to-all(f32[8,64,512]{2,1,0:T(8,128)} %bitcast.7), channel_id=1, replica_groups={{0,2,4,6,8,10,12,14},{1,3,5,7,9,11,13,15},{16,18,20,22,24,26,28,30},{17..., dimensions={0} | all-to-all | bytes 2097152 | tf_op jit(solution)/shard_map/all_to_all | solution.py:374
  79.2 0.9 %unfold.1 = f32[64,2048]{1,0:T(8,128)} custom-call(s32[64,128]{1,0:T(8,128)S(1)} %get-tuple-element.13.label_out, s32[8,2048]{1,0:T(8,128)S(1)} %get-tuple-element.14.keys, f32[8,64,512]{2,1,0:T(8,128)S(1)} %all_to_all.10.parts), custom_call_target="tpu_custom_call" | custom-call | tf_op jit(solution)/shard_map/unfold/pallas_call | solution.py:377
  (3 shorter events, 0.0 us)
Async XLA Ops:
  8.3 30.4 %all-to-all-start = ((bf16[16,128,256]{2,1,0:T(8,128)(2,1)}), bf16[16,128,256]{2,1,0:T(8,128)(2,1)S(1)}, u32[]{:S(2)}, u32[]{:S(2)}) async-start(bf16[16,128,256]{2,1,0:T(8,128)(2,1)} %get-tuple-element.17), calls=%async_computation | async-start | bytes 2097152 | tf_op jit(solution)/shard_map/all_to_all | solution.py:310
  15.7 0.7 copy-start.6
  16.3 0.7 copy-start.9
  17.0 0.7 copy-start.10
  17.7 0.7 copy-start.11
  20.2 0.7 copy-start.5
  20.9 7.6 %copy-start.8 = (s32[16,256]{1,0:T(8,128)}, s32[16,256]{1,0:T(8,128)S(1)}, u32[]{:S(2)}) copy-start(s32[16,256]{1,0:T(8,128)S(1)} %get-tuple-element.15.label_k_hbm) | copy-start | bytes 49156
  20.9 3.4 %copy-start = (bf16[128,16,2048]{2,1,0:T(8,128)(2,1)S(1)}, bf16[128,16,2048]{2,1,0:T(8,128)(2,1)}, u32[]{:S(2)}) copy-start(bf16[128,16,2048]{2,1,0:T(8,128)(2,1)} %w.7) | copy-start | bytes 25165828
  24.3 0.7 copy-start.7
  26.5 3.8 %copy-start.1 = (bf16[16,32,512]{2,1,0:T(8,128)(2,1)}, bf16[16,32,512]{2,1,0:T(8,128)(2,1)S(1)}, u32[]{:S(2)}) copy-start(bf16[16,32,512]{2,1,0:T(8,128)(2,1)S(1)} %fold_couplings.4.refs_0_) | copy-start | bytes 1572868
  26.5 6.0 %collective-permute-start = (bf16[16,32,512]{2,1,0:T(8,128)(2,1)S(1)}, bf16[16,32,512]{2,1,0:T(8,128)(2,1)S(1)}, u32[]{:S(2)}, u32[]{:S(2)}) collective-permute-start(bf16[16,32,512]{2,1,0:T(8,128)(2,1)S(1)} %fold_couplings.4.refs_0_), channel_id=1, source_target_pairs={{0,1},{1,0},{2,3},{3,2},{4,5},{5,4},{6,7},{7,6},{8,9},{9,8},{10,11... | collective-permute-start | bytes 1572872 | tf_op jit(solution)/shard_map/ppermute | solution.py:356
  28.5 3.8 %copy-start.2 = (bf16[16,32,512]{2,1,0:T(8,128)(2,1)}, bf16[16,32,512]{2,1,0:T(8,128)(2,1)S(1)}, u32[]{:S(2)}) copy-start(bf16[16,32,512]{2,1,0:T(8,128)(2,1)S(1)} %fold_couplings.5.refs_1_) | copy-start | bytes 1572868
  28.5 3.9 %collective-permute-start.1 = (bf16[16,32,512]{2,1,0:T(8,128)(2,1)S(1)}, bf16[16,32,512]{2,1,0:T(8,128)(2,1)S(1)}, u32[]{:S(2)}, u32[]{:S(2)}) collective-permute-start(bf16[16,32,512]{2,1,0:T(8,128)(2,1)S(1)} %fold_couplings.5.refs_1_), channel_id=1, source_target_pairs={{0,1},{1,0},{2,3},{3,2},{4,5},{5,4},{6,7},{7,6},{8,9},{9,8},{10,11... | collective-permute-start | bytes 1572872 | tf_op jit(solution)/shard_map/ppermute | solution.py:356
  30.2 8.4 %copy-start.3 = (bf16[16,32,512]{2,1,0:T(8,128)(2,1)}, bf16[16,32,512]{2,1,0:T(8,128)(2,1)S(1)}, u32[]{:S(2)}) copy-start(bf16[16,32,512]{2,1,0:T(8,128)(2,1)S(1)} %fold_couplings.6.refs_2_) | copy-start | bytes 1572868
  30.2 2.2 %collective-permute-start.2 = (bf16[16,32,512]{2,1,0:T(8,128)(2,1)S(1)}, bf16[16,32,512]{2,1,0:T(8,128)(2,1)S(1)}, u32[]{:S(2)}, u32[]{:S(2)}) collective-permute-start(bf16[16,32,512]{2,1,0:T(8,128)(2,1)S(1)} %fold_couplings.6.refs_2_), channel_id=1, source_target_pairs={{0,1},{1,0},{2,3},{3,2},{4,5},{5,4},{6,7},{7,6},{8,9},{9,8},{10,11... | collective-permute-start | bytes 1572872 | tf_op jit(solution)/shard_map/ppermute | solution.py:356
  32.3 6.4 %copy-start.4 = (bf16[16,32,512]{2,1,0:T(8,128)(2,1)}, bf16[16,32,512]{2,1,0:T(8,128)(2,1)S(1)}, u32[]{:S(2)}) copy-start(bf16[16,32,512]{2,1,0:T(8,128)(2,1)S(1)} %fold_couplings.7.refs_3_) | copy-start | bytes 1572868
  32.3 2.1 %collective-permute-start.3 = (bf16[16,32,512]{2,1,0:T(8,128)(2,1)S(1)}, bf16[16,32,512]{2,1,0:T(8,128)(2,1)}, u32[]{:S(2)}, u32[]{:S(2)}) collective-permute-start(bf16[16,32,512]{2,1,0:T(8,128)(2,1)S(1)} %fold_couplings.7.refs_3_), channel_id=1, source_target_pairs={{0,1},{1,0},{2,3},{3,2},{4,5},{5,4},{6,7},{7,6},{8,9},{9,8},{10,11... | collective-permute-start | bytes 1572872 | tf_op jit(solution)/shard_map/ppermute | solution.py:356
  32.5 6.2 %copy-start.13 = (bf16[16,32,512]{2,1,0:T(8,128)(2,1)}, bf16[16,32,512]{2,1,0:T(8,128)(2,1)S(1)}, u32[]{:S(2)}) copy-start(bf16[16,32,512]{2,1,0:T(8,128)(2,1)S(1)} %collective-permute-done.refs_4_) | copy-start | bytes 1572868
  32.5 6.2 %copy-start.14 = (bf16[16,32,512]{2,1,0:T(8,128)(2,1)}, bf16[16,32,512]{2,1,0:T(8,128)(2,1)S(1)}, u32[]{:S(2)}) copy-start(bf16[16,32,512]{2,1,0:T(8,128)(2,1)S(1)} %collective-permute-done.1.refs_5_) | copy-start | bytes 1572868
  32.5 0.9 %copy-start.15 = (bf16[16,32,512]{2,1,0:T(8,128)(2,1)}, bf16[16,32,512]{2,1,0:T(8,128)(2,1)S(1)}, u32[]{:S(2)}) copy-start(bf16[16,32,512]{2,1,0:T(8,128)(2,1)S(1)} %collective-permute-done.2.refs_6_) | copy-start | bytes 1572868
  38.6 1.0 %copy-start.12 = (bf16[16,128,256]{2,1,0:T(8,128)(2,1)}, bf16[16,128,256]{2,1,0:T(8,128)(2,1)S(1)}, u32[]{:S(2)}) copy-start(bf16[16,128,256]{2,1,0:T(8,128)(2,1)S(1)} %all-to-all-done.t_hbm) | copy-start | bytes 3145732

commit v3 on v2

--- a/solution.py
+++ b/solution.py
@@ -10,7 +10,6 @@
 BS = 4
 MOST = 256
 LIMIT = 24 * 1024 * 1024
-MOST_LIMIT = 60 * 1024 * 1024
 F32, BF16, I32 = jnp.float32, jnp.bfloat16, jnp.int32
 
 
@@ -58,74 +57,67 @@
     rows_out,
     sizes_hbm,
     occ_hbm,
-    pair_hbm,
+    pair,
     owner_hbm,
     t_hbm,
-    out,
+    out_hbm,
     place,
     sizes,
     occ,
-    pair,
     owner_row,
     t_vmem,
-    folded_t,
-    target,
-    sems,
+    out,
+    in_sems,
+    out_sems,
 ):
     virtuals = t_hbm.shape[1]
     lanes = 2 * rows
-
-    @pl.when(pl.program_id(0) == 0)
-    def _():
-        pairs = (
-            (owner_hbm, owner_row),
-            (sizes_hbm, sizes),
-            (occ_hbm, occ),
-            (pair_hbm, pair),
-            (t_hbm.at[0], t_vmem),
+    pairs = (
+        (owner_hbm, owner_row),
+        (sizes_hbm, sizes),
+        (occ_hbm, occ),
+        (t_hbm.at[0], t_vmem),
+    )
+    copies = [
+        pltpu.make_async_copy(source, here, in_sems.at[i])
+        for i, (source, here) in enumerate(pairs)
+    ]
+    for copy in copies:
+        copy.start()
+    copies[0].wait()
+    where = block_place(owner_row[...], rows)
+    place[...] = jnp.broadcast_to(where, place.shape)
+    target = jnp.broadcast_to(virtual_place(where, virtuals), (virtuals, lanes))
+    for copy in copies[1:3]:
+        copy.wait()
+    wanted = pair[0] ^ occ[lax.axis_index("vir")]
+    label_e = irrep_of(iota((virtuals, 1), 0), sizes) ^ wanted
+    label_a = irrep_of(iota((1, virtuals), 1), sizes)
+    copies[3].wait()
+    folded = jnp.zeros((virtuals, MOST), F32)
+    for k in range(virtuals // MOST):
+        part = slice(k * MOST, (k + 1) * MOST)
+        folded = folded + jnp.where(
+            label_e == label_a[:, part], t_vmem[:, part].astype(F32), 0.0
         )
-        copies = [
-            pltpu.make_async_copy(source, here, sems.at[i])
-            for i, (source, here) in enumerate(pairs)
-        ]
-        for copy in copies:
-            copy.start()
-        copies[0].wait()
-        where = block_place(owner_row[...], rows)
-        place[...] = jnp.broadcast_to(where, place.shape)
-        target[...] = jnp.broadcast_to(virtual_place(where, virtuals), target.shape)
-        for copy in copies[1:4]:
-            copy.wait()
-        wanted = pair[0] ^ occ[lax.axis_index("vir")]
-        label_e = irrep_of(iota((virtuals, 1), 0), sizes) ^ wanted
-        label_a = irrep_of(iota((1, virtuals), 1), sizes)
-        copies[4].wait()
-        folded = jnp.zeros((virtuals, MOST), F32)
-        for k in range(virtuals // MOST):
-            part = slice(k * MOST, (k + 1) * MOST)
-            folded = folded + jnp.where(
-                label_e == label_a[:, part], t_vmem[:, part].astype(F32), 0.0
-            )
-        folded_t[...] = folded.T.astype(BF16)
-
-    chips = out.shape[0] // 2
-    for chip in range(chips):
-        lane = iota((virtuals, lanes), 1)
-        offset = (pl.program_id(0) * chips + chip) * lanes
-        place = target[:, :1] - offset
+    folded_t = folded.T.astype(BF16)
+    lane = iota((1, lanes), 1)
+
+    def half(values, core):
+        return jnp.concatenate(
+            [
+                values[start : start + rows_out]
+                for start in range(core * rows_out, MOST, 2 * rows_out)
+            ],
+            axis=0,
+        )
+
+    sends = []
+    for chip in range(out.shape[0] // 2):
 
         def moved(flip):
-            hot = jnp.where(place == lane ^ flip, 1.0, 0.0).astype(BF16)
-            return jnp.dot(folded_t[...], hot, preferred_element_type=F32)
-
-        def half(values, core):
-            return jnp.concatenate(
-                [
-                    values[start : start + rows_out]
-                    for start in range(core * rows_out, MOST, 2 * rows_out)
-                ],
-                axis=0,
-            )
+            hot = jnp.where(target == (lane ^ flip) + chip * lanes, 1.0, 0.0).astype(BF16)
+            return jnp.dot(folded_t, hot, preferred_element_type=F32)
 
         here = moved(0)
         out[2 * chip] = half(here, 0).astype(BF16)
@@ -135,6 +127,11 @@
             out[2 * chip + 1, :, rows:] = there[:, :rows].astype(BF16)
         else:
             out[2 * chip + 1] = half(moved(rows), 1).astype(BF16)
+        both = pl.ds(2 * chip, 2)
+        sends.append(pltpu.make_async_copy(out.at[both], out_hbm.at[both], out_sems.at[chip]))
+        sends[-1].start()
+    for copy in sends:
+        copy.wait()
 
 
 def label_kernel(
@@ -193,65 +190,54 @@
             ].astype(BF16)
 
 
-def product_kernel(label_k_hbm, label_kept_hbm, t_hbm, *refs):
-    *pieces, out, label_k, label_kept, t, w, sems = refs
+def product_kernel(pieces, label_k, label_kept, t, *refs):
+    own, mate_hbm, (out, mate, sems) = refs[:pieces], refs[pieces : 2 * pieces], refs[2 * pieces :]
     occupied, half, lanes = t.shape
+    rows = lanes // 2
     kept = out.shape[0]
-    size = pieces[0].shape[1]
-    m_block = max(1, min(occupied, 1024 // lanes))
-    steps = occupied // m_block
-
-    def fetches(step):
-        part = pl.ds(step * m_block, m_block)
-        pairs = [(t_hbm.at[part], t.at[part])] + [
-            (piece.at[part], w.at[part, pl.ds(i * size, size)])
-            for i, piece in enumerate(pieces)
-        ]
-        return [
-            pltpu.make_async_copy(source, here, sems.at[2 + step * len(pairs) + i])
-            for i, (source, here) in enumerate(pairs)
-        ]
-
-    tables = [
-        pltpu.make_async_copy(label_k_hbm, label_k, sems.at[0]),
-        pltpu.make_async_copy(label_kept_hbm, label_kept, sems.at[1]),
+    size = rows // pieces
+    copies = [
+        pltpu.make_async_copy(mate_hbm[i], mate.at[:, i * size : (i + 1) * size], sems.at[i])
+        for i in range(pieces)
     ]
-    for copy in tables:
+    for copy in copies:
         copy.start()
-    for step in range(steps):
-        for copy in fetches(step):
-            copy.start()
+    wide_label = jnp.broadcast_to(label_kept[:, :1], (kept, rows))
     out[...] = jnp.zeros(out.shape, F32)
-    for copy in tables:
+    m_block = max(1, min(occupied, 1024 // rows))
+
+    def accumulate(side, couplings):
+        lane = slice(side * rows, (side + 1) * rows)
+
+        @pl.loop(0, occupied // m_block)
+        def _(step):
+            left, right = [], []
+            for i in range(m_block):
+                m = step * m_block + i
+                wanted = label_k[pl.ds(m, 1), :][:, lane]
+                values = t[m][:, lane].astype(F32)
+                left.append(
+                    jnp.concatenate(
+                        [
+                            jnp.where(wide_label[k : k + half] == wanted, values, 0.0).astype(BF16)
+                            for k in range(0, kept, half)
+                        ],
+                        axis=0,
+                    )
+                )
+                right.append(couplings(m))
+            if rows % 128 == 0:
+                left = [jnp.concatenate(left, axis=1)]
+                right = [jnp.concatenate(right, axis=0)]
+            total = jnp.dot(left[0], right[0], preferred_element_type=F32)
+            for x, y in zip(left[1:], right[1:]):
+                total = total + jnp.dot(x, y, preferred_element_type=F32)
+            out[...] += total
+
+    accumulate(0, lambda m: jnp.concatenate([piece[m] for piece in own], axis=0))
+    for copy in copies:
         copy.wait()
-    wide_label = jnp.broadcast_to(label_kept[:, :1], (kept, lanes))
-
-    @pl.loop(0, steps)
-    def _(step):
-        for copy in fetches(step):
-            copy.wait()
-        left, right = [], []
-        for i in range(m_block):
-            m = step * m_block + i
-            wanted = label_k[pl.ds(m, 1), :]
-            values = t[m].astype(F32)
-            left.append(
-                jnp.concatenate(
-                    [
-                        jnp.where(wide_label[k : k + half] == wanted, values, 0.0).astype(BF16)
-                        for k in range(0, kept, half)
-                    ],
-                    axis=0,
-                )
-            )
-            right.append(w[m])
-        if lanes % 128 == 0:
-            left = [jnp.concatenate(left, axis=1)]
-            right = [jnp.concatenate(right, axis=0)]
-        total = jnp.dot(left[0], right[0], preferred_element_type=F32)
-        for x, y in zip(left[1:], right[1:]):
-            total = total + jnp.dot(x, y, preferred_element_type=F32)
-        out[...] += total
+    accumulate(1, lambda m: mate[m])
 
 
 def finish_kernel(label_out, keys, parts, out):
@@ -263,6 +249,10 @@
         out[:, k : k + wide] = jnp.where(
             label_out[:, :1] == keys[:1, k : k + wide], total, 0.0
         )
+
+
+in_hbm = functools.partial(pltpu.with_memory_space_constraint, memory_space=pltpu.HBM)
+in_vmem = functools.partial(pltpu.with_memory_space_constraint, memory_space=pltpu.VMEM)
 
 
 def per_device(amplitudes, couplings, occ_irrep, pair_irrep, j_irrep, block_sizes, owner):
@@ -279,34 +269,33 @@
     vmem = pl.BlockSpec(memory_space=pltpu.VMEM)
     hbm = pl.BlockSpec(memory_space=pltpu.HBM)
     params = pltpu.CompilerParams(vmem_limit_bytes=LIMIT)
-    alone = pltpu.CompilerParams(vmem_limit_bytes=MOST_LIMIT)
-
-    chips_step = max(1, 256 // lanes)
+
     outgoing, place = pl.pallas_call(
         functools.partial(pack_kernel, rows, rows_out),
         out_shape=(
-            jax.ShapeDtypeStruct((devices, MOST // 2, lanes), BF16),
+            pltpu.HBM((devices, MOST // 2, lanes), BF16),
             jax.ShapeDtypeStruct((8, blocks), I32),
         ),
-        grid=(chips // chips_step,),
-        in_specs=[hbm] * 5,
-        out_specs=(
-            pl.BlockSpec((2 * chips_step, MOST // 2, lanes), lambda i: (i, 0, 0)),
-            pl.BlockSpec((8, blocks), lambda i: (0, 0)),
-        ),
+        in_specs=[hbm, hbm, smem, hbm, hbm],
+        out_specs=(hbm, vmem),
         scratch_shapes=[
             pltpu.SMEM(block_sizes.shape, I32),
             pltpu.SMEM(occ_irrep.shape, I32),
-            pltpu.SMEM(pair_irrep.shape, I32),
             pltpu.VMEM((1, blocks), I32),
             pltpu.VMEM((virtuals, virtuals), BF16),
-            pltpu.VMEM((MOST, virtuals), BF16),
-            pltpu.VMEM((virtuals, 128), I32),
-            pltpu.SemaphoreType.DMA((5,)),
+            pltpu.VMEM((devices, MOST // 2, lanes), BF16),
+            pltpu.SemaphoreType.DMA((4,)),
+            pltpu.SemaphoreType.DMA((chips,)),
         ],
-        compiler_params=alone,
+        compiler_params=params,
         name="pack_amplitudes",
-    )(block_sizes, occ_irrep, pair_irrep, owner.reshape(1, blocks), amplitudes)
+    )(
+        in_hbm(block_sizes),
+        in_hbm(occ_irrep),
+        pair_irrep,
+        in_hbm(owner.reshape(1, blocks)),
+        in_hbm(amplitudes),
+    )
     received = lax.all_to_all(outgoing, "vir", 0, 0)
 
     label_row, label_k, label_kept, label_out, keys = pl.pallas_call(
@@ -351,25 +340,25 @@
                     transcendentals=0,
                 ),
                 name="fold_couplings",
-            )(occ_irrep, label_row.reshape(rows), keys, couplings)
+            )(occ_irrep, label_row.reshape(rows), keys, in_hbm(couplings))
         )
         w_mate.append(lax.ppermute(w_own[-1], "vir", [(d, d ^ 1) for d in range(devices)]))
 
     partial = pl.pallas_call(
-        product_kernel,
+        functools.partial(product_kernel, pieces),
         out_shape=jax.ShapeDtypeStruct((kept, wide), F32),
-        in_specs=[hbm] * (3 + 2 * pieces),
+        in_specs=[vmem] * (3 + pieces) + [hbm] * pieces,
         out_specs=vmem,
         scratch_shapes=[
-            pltpu.VMEM((occupied, lanes), I32),
-            pltpu.VMEM((kept, 128), I32),
-            pltpu.VMEM(received.shape, BF16),
-            pltpu.VMEM((occupied, lanes, wide), BF16),
-            pltpu.SemaphoreType.DMA((2 + occupied * (1 + 2 * pieces),)),
+            pltpu.VMEM((occupied, rows, wide), BF16),
+            pltpu.SemaphoreType.DMA((pieces,)),
         ],
-        compiler_params=alone,
+        compiler_params=params,
         name="multiply",
-    )(label_k, label_kept, received, *w_own, *w_mate)
+    )(
+        *[in_vmem(x) for x in (label_k, label_kept, received, *w_own)],
+        *[in_hbm(x) for x in w_mate],
+    )
     sides = [[d for d in range(devices) if d % 2 == core] for core in (0, 1)]
     parts = lax.all_to_all(
         partial.reshape(chips, rows_out, wide), "vir", 0, 0, axis_index_groups=sides

time: 80.5 us -> 73 us (0.907)
  local copies, waits for them, and re-layouts: 9.24 us -> 4.39 us
  Pallas kernels: 23.1 us -> 19.6 us
  waiting for transfers between devices: 5.3 us -> 6.41 us
    unnamed x32 -> x14, local copies, waits for them, and re-layouts: 9.24 us -> 4.39 us
    pallas_call x1, Pallas kernels: 6.65 us -> 3.12 us  [per_device(): pl.pallas_call(functools.partial(product_kernel, pieces), out_shape=jax.S...]
    pallas_call x1, Pallas kernels: 7.61 us -> 4.78 us  [per_device(): pl.pallas_call(functools.partial(pack_kernel, rows, rows_out), out_shape=...]
    pallas_call x4, Pallas kernels: 6.12 us -> 8.93 us  [per_device(): pl.pallas_call(functools.partial(fold_kernel, first), out_shape=jax.Shape...]
    all_to_all x1, waiting for transfers between devices: 4.24 us -> 6.28 us  [per_device(): received = lax.all_to_all(outgoing, 'vir', 0, 0)]
    ppermute x4, waiting for transfers between devices: 1.06 us -> 0.14 us  [per_device(): lax.ppermute(w_own[-1], 'vir', [(d, d ^ 1) for d in range(devices)])]
  transfers between devices with their start and end apart: 5 -> 5, of which waited for: 2 -> 2; matrix products, arithmetic and copies ran while one was open for 0% -> 0% of each run, Pallas kernels for 10% -> 15%
where the time goes in v3:
time: 73 us; the launch traced here: 72.5 us
  blocking collectives  32.7 us (45%)
  Pallas kernels  19.6 us (27%)
  starting transfers between devices  8.68 us (12%)
  waiting for transfers between devices  6.41 us (9%)
  local copies, waits for them, and re-layouts  4.39 us (6%)
  between operations  0.76 us (1%)
    all_to_all x1, blocking collectives, per_device(): lax.all_to_all(partial.reshape(chips, rows_out, wide), 'vir', 0, 0, axis_...  32.7 us
    pallas_call x4, Pallas kernels, per_device(): pl.pallas_call(functools.partial(fold_kernel, first), out_shape=jax.Shape...  8.93 us
    all_to_all x1, starting transfers between devices, per_device(): received = lax.all_to_all(outgoing, 'vir', 0, 0)  7.4 us
    all_to_all x1, waiting for transfers between devices, per_device(): received = lax.all_to_all(outgoing, 'vir', 0, 0)  6.28 us
    pallas_call x1, Pallas kernels, per_device(): pl.pallas_call(functools.partial(pack_kernel, rows, rows_out), out_shape=...  4.78 us
    unnamed x14, local copies, waits for them, and re-layouts  4.39 us
    pallas_call x1, Pallas kernels, per_device(): pl.pallas_call(functools.partial(product_kernel, pieces), out_shape=jax.S...  3.12 us
    pallas_call x1, Pallas kernels, per_device(): pl.pallas_call(functools.partial(label_kernel, rows, rows_out), out_shape...  1.84 us
  transfers between devices with their start and end apart: 5, of which 2 were waited for; matrix products, arithmetic and copies ran while one was open for 0% of the time, Pallas kernels for 15%

profile of v3, /device:TPU:0, one launch (start us, length us, event | category | flops | bytes accessed | tf_op | source)
XLA Modules:
  0.0 72.5 jit_solution(9695873839243383086)
XLA Ops:
  0.7 4.8 %pack_amplitudes.1 = (bf16[16,128,256]{2,1,0:T(8,128)(2,1)}, s32[8,256]{1,0:T(8,128)S(1)}) custom-call(s32[8]{0:T(128)} %sizes.1, s32[16]{0:T(128)} %occ.9, s32[1]{0:T(128)S(6)} %copy.8.pair, s32[1,256]{1,0:T(1,128)} %bitcast.8, bf16[1,1024,1024]{2,1,0:T(8,128)(2,1)} %t_hbm.1), custom_call_target="tpu_custom_call" | custom-call | tf_op jit(solution)/shard_map/pack_amplitudes/pallas_call | solution.py:273
  5.4 7.4 %all-to-all-start = ((bf16[16,128,256]{2,1,0:T(8,128)(2,1)}), bf16[16,128,256]{2,1,0:T(8,128)(2,1)S(1)}, u32[]{:S(2)}, u32[]{:S(2)}) async-start(bf16[16,128,256]{2,1,0:T(8,128)(2,1)} %get-tuple-element.17), calls=%async_computation | async-start | bytes 2097152 | tf_op jit(solution)/shard_map/all_to_all | solution.py:299
  12.8 0.0 copy-start
  12.9 0.6 copy-done
  13.5 0.0 copy-start.2
  13.5 0.7 copy-done.2
  14.2 0.0 copy-start.3
  14.2 0.7 copy-done.3
  14.8 1.8 %labels.1 = (s32[1,128]{1,0:T(1,128)S(1)}, s32[16,256]{1,0:T(8,128)S(1)}, s32[512,128]{1,0:T(8,128)S(1)}, s32[64,128]{1,0:T(8,128)S(1)}, s32[8,2048]{1,0:T(8,128)S(1)}) custom-call(s32[8]{0:T(128)S(1)} %copy-done.2, s32[16]{0:T(128)S(1)} %copy-done, s32[1]{0:T(128)S(6)} %copy.8.pair, s32[2]{0:T(128)S(1)} %copy-done.3, s32[8,256]{1,0:T(8,128)S(1)} %get-tuple-element.12.place), custom_call_target="tpu_custom_call" | custom-call | tf_op jit(solution)/shard_map/labels/pallas_call | solution.py:301
  16.7 0.0 copy-start.1
  16.7 0.6 copy-done.1
  17.3 2.2 %fold_couplings.4.refs_0_ = bf16[16,32,512]{2,1,0:T(8,128)(2,1)S(1)} custom-call(s32[16]{0:T(128)S(1)} %copy-done.1, s32[128]{0:T(128)S(1)} %bitcast.4, s32[8,2048]{1,0:T(8,128)S(1)} %get-tuple-element.14.keys, bf16[128,16,2048]{2,1,0:T(8,128)(2,1)} %w.7), custom_call_target="tpu_custom_call" | custom-call | flops 4194304 | bytes 3145728 | tf_op jit(solution)/shard_map/fold_couplings/pallas_call | solution.py:323
  19.6 0.5 collective-permute-start
  20.0 2.2 %fold_couplings.5.refs_1_ = bf16[16,32,512]{2,1,0:T(8,128)(2,1)S(1)} custom-call(s32[16]{0:T(128)S(1)} %copy-done.1, s32[128]{0:T(128)S(1)} %bitcast.5, s32[8,2048]{1,0:T(8,128)S(1)} %get-tuple-element.14.keys, bf16[128,16,2048]{2,1,0:T(8,128)(2,1)} %w.7), custom_call_target="tpu_custom_call" | custom-call | flops 4194304 | bytes 3145728 | tf_op jit(solution)/shard_map/fold_couplings/pallas_call | solution.py:323
  22.3 0.2 collective-permute-start.1
  22.4 2.2 %fold_couplings.6.refs_2_ = bf16[16,32,512]{2,1,0:T(8,128)(2,1)S(1)} custom-call(s32[16]{0:T(128)S(1)} %copy-done.1, s32[128]{0:T(128)S(1)} %bitcast.6, s32[8,2048]{1,0:T(8,128)S(1)} %get-tuple-element.14.keys, bf16[128,16,2048]{2,1,0:T(8,128)(2,1)} %w.7), custom_call_target="tpu_custom_call" | custom-call | flops 4194304 | bytes 3145728 | tf_op jit(solution)/shard_map/fold_couplings/pallas_call | solution.py:323
  24.7 0.5 collective-permute-start.2
  25.2 2.2 %fold_couplings.7.refs_3_ = bf16[16,32,512]{2,1,0:T(8,128)(2,1)S(1)} custom-call(s32[16]{0:T(128)S(1)} %copy-done.1, s32[128]{0:T(128)S(1)} %bitcast.7, s32[8,2048]{1,0:T(8,128)S(1)} %get-tuple-element.14.keys, bf16[128,16,2048]{2,1,0:T(8,128)(2,1)} %w.7), custom_call_target="tpu_custom_call" | custom-call | flops 4194304 | bytes 3145728 | tf_op jit(solution)/shard_map/fold_couplings/pallas_call | solution.py:323
  27.4 0.2 collective-permute-start.3
  27.6 0.0 collective-permute-done.refs_4_
  27.6 0.0 copy-start.4
  27.6 0.0 collective-permute-done.1.refs_5_
  27.6 0.0 copy-start.5
  27.6 0.0 collective-permute-done.2.refs_6_
  27.6 0.8 %copy-done.4 = bf16[16,32,512]{2,1,0:T(8,128)(2,1)} copy-done((bf16[16,32,512]{2,1,0:T(8,128)(2,1)}, bf16[16,32,512]{2,1,0:T(8,128)(2,1)S(1)}, u32[]{:S(2)}) %copy-start.4) | copy-done | bytes 524312
  28.4 0.2 copy-done.5
  28.6 0.0 copy-start.6
  28.6 0.8 %copy-done.6 = bf16[16,32,512]{2,1,0:T(8,128)(2,1)} copy-done((bf16[16,32,512]{2,1,0:T(8,128)(2,1)}, bf16[16,32,512]{2,1,0:T(8,128)(2,1)S(1)}, u32[]{:S(2)}) %copy-start.6) | copy-done | bytes 524312
  29.4 0.1 collective-permute-done.3.refs_7_
  29.5 6.3 %all-to-all-done.t = bf16[16,128,256]{2,1,0:T(8,128)(2,1)S(1)} async-done(((bf16[16,128,256]{2,1,0:T(8,128)(2,1)}), bf16[16,128,256]{2,1,0:T(8,128)(2,1)S(1)}, u32[]{:S(2)}, u32[]{:S(2)}) %all-to-all-start) | async-done | bytes 1048608 | tf_op jit(solution)/shard_map/all_to_all | solution.py:299
  35.8 3.1 %multiply.1 = f32[512,512]{1,0:T(8,128)S(1)} custom-call(s32[16,256]{1,0:T(8,128)S(1)} %get-tuple-element.15.label_k, s32[512,128]{1,0:T(8,128)S(1)} %get-tuple-element.16.label_kept, bf16[16,128,256]{2,1,0:T(8,128)(2,1)S(1)} %all-to-all-done.t, bf16[16,32,512]{2,1,0:T(8,128)(2,1)S(1)} %fold_couplings.4.refs_0_, ...), custom_call_target="tpu_custom_call" | custom-call | tf_op jit(solution)/shard_map/multiply/pallas_call | solution.py:347
  38.9 32.7 %all_to_all.10.parts = f32[8,64,512]{2,1,0:T(8,128)S(1)} all-to-all(f32[8,64,512]{2,1,0:T(8,128)S(1)} %bitcast.3), channel_id=1, replica_groups={{0,2,4,6,8,10,12,14},{1,3,5,7,9,11,13,15},{16,18,20,22,24,26,28,30},{17..., dimensions={0} | all-to-all | bytes 2097152 | tf_op jit(solution)/shard_map/all_to_all | solution.py:363
  71.7 0.9 %unfold.1 = f32[64,2048]{1,0:T(8,128)} custom-call(s32[64,128]{1,0:T(8,128)S(1)} %get-tuple-element.13.label_out, s32[8,2048]{1,0:T(8,128)S(1)} %get-tuple-element.14.keys, f32[8,64,512]{2,1,0:T(8,128)S(1)} %all_to_all.10.parts), custom_call_target="tpu_custom_call" | custom-call | tf_op jit(solution)/shard_map/unfold/pallas_call | solution.py:366
Async XLA Ops:
  5.4 30.3 %all-to-all-start = ((bf16[16,128,256]{2,1,0:T(8,128)(2,1)}), bf16[16,128,256]{2,1,0:T(8,128)(2,1)S(1)}, u32[]{:S(2)}, u32[]{:S(2)}) async-start(bf16[16,128,256]{2,1,0:T(8,128)(2,1)} %get-tuple-element.17), calls=%async_computation | async-start | bytes 2097152 | tf_op jit(solution)/shard_map/all_to_all | solution.py:299
  12.8 0.7 copy-start
  13.5 0.7 copy-start.2
  14.2 0.7 copy-start.3
  16.7 0.7 copy-start.1
  19.6 8.0 %collective-permute-start = (bf16[16,32,512]{2,1,0:T(8,128)(2,1)S(1)}, bf16[16,32,512]{2,1,0:T(8,128)(2,1)S(1)}, u32[]{:S(2)}, u32[]{:S(2)}) collective-permute-start(bf16[16,32,512]{2,1,0:T(8,128)(2,1)S(1)} %fold_couplings.4.refs_0_), channel_id=1, source_target_pairs={{0,1},{1,0},{2,3},{3,2},{4,5},{5,4},{6,7},{7,6},{8,9},{9,8},{10,11... | collective-permute-start | bytes 1572872 | tf_op jit(solution)/shard_map/ppermute | solution.py:345
  22.3 5.3 %collective-permute-start.1 = (bf16[16,32,512]{2,1,0:T(8,128)(2,1)S(1)}, bf16[16,32,512]{2,1,0:T(8,128)(2,1)S(1)}, u32[]{:S(2)}, u32[]{:S(2)}) collective-permute-start(bf16[16,32,512]{2,1,0:T(8,128)(2,1)S(1)} %fold_couplings.5.refs_1_), channel_id=1, source_target_pairs={{0,1},{1,0},{2,3},{3,2},{4,5},{5,4},{6,7},{7,6},{8,9},{9,8},{10,11... | collective-permute-start | bytes 1572872 | tf_op jit(solution)/shard_map/ppermute | solution.py:345
  24.7 2.9 %collective-permute-start.2 = (bf16[16,32,512]{2,1,0:T(8,128)(2,1)S(1)}, bf16[16,32,512]{2,1,0:T(8,128)(2,1)S(1)}, u32[]{:S(2)}, u32[]{:S(2)}) collective-permute-start(bf16[16,32,512]{2,1,0:T(8,128)(2,1)S(1)} %fold_couplings.6.refs_2_), channel_id=1, source_target_pairs={{0,1},{1,0},{2,3},{3,2},{4,5},{5,4},{6,7},{7,6},{8,9},{9,8},{10,11... | collective-permute-start | bytes 1572872 | tf_op jit(solution)/shard_map/ppermute | solution.py:345
  27.4 2.1 %collective-permute-start.3 = (bf16[16,32,512]{2,1,0:T(8,128)(2,1)S(1)}, bf16[16,32,512]{2,1,0:T(8,128)(2,1)}, u32[]{:S(2)}, u32[]{:S(2)}) collective-permute-start(bf16[16,32,512]{2,1,0:T(8,128)(2,1)S(1)} %fold_couplings.7.refs_3_), channel_id=1, source_target_pairs={{0,1},{1,0},{2,3},{3,2},{4,5},{5,4},{6,7},{7,6},{8,9},{9,8},{10,11... | collective-permute-start | bytes 1572872 | tf_op jit(solution)/shard_map/ppermute | solution.py:345
  27.6 0.8 %copy-start.4 = (bf16[16,32,512]{2,1,0:T(8,128)(2,1)}, bf16[16,32,512]{2,1,0:T(8,128)(2,1)S(1)}, u32[]{:S(2)}) copy-start(bf16[16,32,512]{2,1,0:T(8,128)(2,1)S(1)} %collective-permute-done.refs_4_) | copy-start | bytes 1572868
  27.6 1.0 %copy-start.5 = (bf16[16,32,512]{2,1,0:T(8,128)(2,1)}, bf16[16,32,512]{2,1,0:T(8,128)(2,1)S(1)}, u32[]{:S(2)}) copy-start(bf16[16,32,512]{2,1,0:T(8,128)(2,1)S(1)} %collective-permute-done.1.refs_5_) | copy-start | bytes 1572868
  28.6 0.8 %copy-start.6 = (bf16[16,32,512]{2,1,0:T(8,128)(2,1)}, bf16[16,32,512]{2,1,0:T(8,128)(2,1)S(1)}, u32[]{:S(2)}) copy-start(bf16[16,32,512]{2,1,0:T(8,128)(2,1)S(1)} %collective-permute-done.2.refs_6_) | copy-start | bytes 1572868

commit v4 on v3

--- a/solution.py
+++ b/solution.py
@@ -10,7 +10,11 @@
 BS = 4
 MOST = 256
 LIMIT = 24 * 1024 * 1024
-F32, BF16, I32 = jnp.float32, jnp.bfloat16, jnp.int32
+F32, BF16, I32, I16 = jnp.float32, jnp.bfloat16, jnp.int32, jnp.int16
+TOP = 32767.0
+STEPS = 256.0
+SMALL = 2.0**-126
+PAD = 16
 
 
 def irrep_of(index, sizes):
@@ -191,7 +195,8 @@
 
 
 def product_kernel(pieces, label_k, label_kept, t, *refs):
-    own, mate_hbm, (out, mate, sems) = refs[:pieces], refs[pieces : 2 * pieces], refs[2 * pieces :]
+    own, mate_hbm = refs[:pieces], refs[pieces : 2 * pieces]
+    coded, out, mate, sems = refs[2 * pieces :]
     occupied, half, lanes = t.shape
     rows = lanes // 2
     kept = out.shape[0]
@@ -238,13 +243,44 @@
     for copy in copies:
         copy.wait()
     accumulate(1, lambda m: mate[m])
+    rows_out = kept // coded.shape[0]
+    for chip in range(coded.shape[0]):
+        coded[chip] = encode(out[chip * rows_out : (chip + 1) * rows_out, :])
+
+
+def encode(values):
+    row = iota((PAD, 128), 0)
+    scales = jnp.zeros((PAD, 128), I32)
+    blocks = []
+    for i in range(values.shape[1] // 128):
+        part = values[:, i * 128 : (i + 1) * 128]
+        largest = jnp.maximum(jnp.max(jnp.abs(part), axis=0, keepdims=True), SMALL)
+        scale = jnp.floor(jnp.log2(largest) * STEPS) + 2.0
+        factor = jnp.exp2(scale * (-0.5 / STEPS))
+        blocks.append(jnp.floor(part * factor * (factor * TOP) + 0.5).astype(I32))
+        scales = jnp.where(row == i, scale.astype(I32), scales)
+    return jnp.concatenate(blocks + [scales], axis=0).astype(I16)
+
+
+def decode(coded, rows_out):
+    values = coded.astype(I32)
+    blocks = []
+    for i in range((coded.shape[0] - PAD) // rows_out):
+        scale = values[coded.shape[0] - PAD + i :][:1].astype(F32)
+        factor = jnp.exp2(scale * (0.5 / STEPS))
+        part = values[i * rows_out : (i + 1) * rows_out].astype(F32)
+        blocks.append(part * (factor * (1.0 / TOP)) * factor)
+    return blocks
 
 
 def finish_kernel(label_out, keys, parts, out):
-    chips, rows_out, wide = parts.shape
-    total = parts[0]
+    chips = parts.shape[0]
+    rows_out = out.shape[0]
+    total = decode(parts[0], rows_out)
     for q in range(1, chips):
-        total = total + parts[q]
+        total = [x + y for x, y in zip(total, decode(parts[q], rows_out))]
+    total = jnp.concatenate(total, axis=1)
+    wide = total.shape[1]
     for k in range(0, out.shape[1], wide):
         out[:, k : k + wide] = jnp.where(
             label_out[:, :1] == keys[:1, k : k + wide], total, 0.0
@@ -346,10 +382,11 @@
 
     partial = pl.pallas_call(
         functools.partial(product_kernel, pieces),
-        out_shape=jax.ShapeDtypeStruct((kept, wide), F32),
+        out_shape=jax.ShapeDtypeStruct((chips, wide // 128 * rows_out + PAD, 128), I16),
         in_specs=[vmem] * (3 + pieces) + [hbm] * pieces,
         out_specs=vmem,
         scratch_shapes=[
+            pltpu.VMEM((kept, wide), F32),
             pltpu.VMEM((occupied, rows, wide), BF16),
             pltpu.SemaphoreType.DMA((pieces,)),
         ],
@@ -360,9 +397,7 @@
         *[in_hbm(x) for x in w_mate],
     )
     sides = [[d for d in range(devices) if d % 2 == core] for core in (0, 1)]
-    parts = lax.all_to_all(
-        partial.reshape(chips, rows_out, wide), "vir", 0, 0, axis_index_groups=sides
-    )
+    parts = lax.all_to_all(partial, "vir", 0, 0, axis_index_groups=sides)
     return pl.pallas_call(
         finish_kernel,
         out_shape=jax.ShapeDtypeStruct((rows_out, columns), F32),

time: 73 us -> 63.6 us (0.87)
  blocking collectives: 32.7 us -> 23 us
    all_to_all x1, blocking collectives: 32.7 us -> 23 us  [per_device(): parts = lax.all_to_all(partial, 'vir', 0, 0, axis_index_groups=sides)]
  transfers between devices with their start and end apart: 5 -> 5, of which waited for: 2 -> 2; matrix products, arithmetic and copies ran while one was open for 0% -> 0% of each run, Pallas kernels for 15% -> 17%
where the time goes in v4:
time: 63.6 us; the launch traced here: 63.3 us
  blocking collectives  23 us (36%)
  Pallas kernels  20 us (31%)
  starting transfers between devices  8.68 us (14%)
  waiting for transfers between devices  6.41 us (10%)
  local copies, waits for them, and re-layouts  4.39 us (7%)
  between operations  0.76 us (1%)
    all_to_all x1, blocking collectives, per_device(): parts = lax.all_to_all(partial, 'vir', 0, 0, axis_index_groups=sides)  23 us
    pallas_call x4, Pallas kernels, per_device(): pl.pallas_call(functools.partial(fold_kernel, first), out_shape=jax.Shape...  8.93 us
    all_to_all x1, starting transfers between devices, per_device(): received = lax.all_to_all(outgoing, 'vir', 0, 0)  7.4 us
    all_to_all x1, waiting for transfers between devices, per_device(): received = lax.all_to_all(outgoing, 'vir', 0, 0)  6.28 us
    pallas_call x1, Pallas kernels, per_device(): pl.pallas_call(functools.partial(pack_kernel, rows, rows_out), out_shape=...  4.78 us
    unnamed x14, local copies, waits for them, and re-layouts  4.39 us
    pallas_call x1, Pallas kernels, per_device(): pl.pallas_call(functools.partial(product_kernel, pieces), out_shape=jax.S...  3.47 us
    pallas_call x1, Pallas kernels, per_device(): pl.pallas_call(functools.partial(label_kernel, rows, rows_out), out_shape...  1.84 us
  transfers between devices with their start and end apart: 5, of which 2 were waited for; matrix products, arithmetic and copies ran while one was open for 0% of the time, Pallas kernels for 17%

profile of v4, /device:TPU:0, one launch (start us, length us, event | category | flops | bytes accessed | tf_op | source)
XLA Modules:
  0.0 63.3 jit_solution(8012449463328387219)
XLA Ops:
  0.7 4.8 %pack_amplitudes.1 = (bf16[16,128,256]{2,1,0:T(8,128)(2,1)}, s32[8,256]{1,0:T(8,128)S(1)}) custom-call(s32[8]{0:T(128)} %sizes.1, s32[16]{0:T(128)} %occ.9, s32[1]{0:T(128)S(6)} %copy.8.pair, s32[1,256]{1,0:T(1,128)} %bitcast.6, bf16[1,1024,1024]{2,1,0:T(8,128)(2,1)} %t_hbm.1), custom_call_target="tpu_custom_call" | custom-call | tf_op jit(solution)/shard_map/pack_amplitudes/pallas_call | solution.py:309
  5.4 7.4 %all-to-all-start = ((bf16[16,128,256]{2,1,0:T(8,128)(2,1)}), bf16[16,128,256]{2,1,0:T(8,128)(2,1)S(1)}, u32[]{:S(2)}, u32[]{:S(2)}) async-start(bf16[16,128,256]{2,1,0:T(8,128)(2,1)} %get-tuple-element.17), calls=%async_computation | async-start | bytes 2097152 | tf_op jit(solution)/shard_map/all_to_all | solution.py:335
  12.8 0.0 copy-start
  12.9 0.6 %copy-done = s32[16]{0:T(128)S(1)} copy-done((s32[16]{0:T(128)S(1)}, s32[16]{0:T(128)}, u32[]{:S(2)}) %copy-start) | copy-done | bytes 88
  13.5 0.0 copy-start.2
  13.5 0.7 %copy-done.2 = s32[8]{0:T(128)S(1)} copy-done((s32[8]{0:T(128)S(1)}, s32[8]{0:T(128)}, u32[]{:S(2)}) %copy-start.2) | copy-done | bytes 56
  14.2 0.0 copy-start.3
  14.2 0.7 %copy-done.3 = s32[2]{0:T(128)S(1)} copy-done((s32[2]{0:T(128)S(1)}, s32[2]{0:T(128)}, u32[]{:S(2)}) %copy-start.3) | copy-done | bytes 32
  14.8 1.8 %labels.1 = (s32[1,128]{1,0:T(1,128)S(1)}, s32[16,256]{1,0:T(8,128)S(1)}, s32[512,128]{1,0:T(8,128)S(1)}, s32[64,128]{1,0:T(8,128)S(1)}, s32[8,2048]{1,0:T(8,128)S(1)}) custom-call(s32[8]{0:T(128)S(1)} %copy-done.2, s32[16]{0:T(128)S(1)} %copy-done, s32[1]{0:T(128)S(6)} %copy.8.pair, s32[2]{0:T(128)S(1)} %copy-done.3, s32[8,256]{1,0:T(8,128)S(1)} %get-tuple-element.12.place), custom_call_target="tpu_custom_call" | custom-call | tf_op jit(solution)/shard_map/labels/pallas_call | solution.py:337
  16.7 0.0 copy-start.1
  16.7 0.6 %copy-done.1 = s32[16]{0:T(128)S(1)} copy-done((s32[16]{0:T(128)S(1)}, s32[16]{0:T(128)}, u32[]{:S(2)}) %copy-start.1) | copy-done | bytes 88
  17.3 2.2 %fold_couplings.4.refs_0_ = bf16[16,32,512]{2,1,0:T(8,128)(2,1)S(1)} custom-call(s32[16]{0:T(128)S(1)} %copy-done.1, s32[128]{0:T(128)S(1)} %bitcast.2, s32[8,2048]{1,0:T(8,128)S(1)} %get-tuple-element.14.keys, bf16[128,16,2048]{2,1,0:T(8,128)(2,1)} %w.7), custom_call_target="tpu_custom_call" | custom-call | flops 4194304 | bytes 3145728 | tf_op jit(solution)/shard_map/fold_couplings/pallas_call | solution.py:359
  19.6 0.5 collective-permute-start
  20.0 2.2 %fold_couplings.5.refs_1_ = bf16[16,32,512]{2,1,0:T(8,128)(2,1)S(1)} custom-call(s32[16]{0:T(128)S(1)} %copy-done.1, s32[128]{0:T(128)S(1)} %bitcast.3, s32[8,2048]{1,0:T(8,128)S(1)} %get-tuple-element.14.keys, bf16[128,16,2048]{2,1,0:T(8,128)(2,1)} %w.7), custom_call_target="tpu_custom_call" | custom-call | flops 4194304 | bytes 3145728 | tf_op jit(solution)/shard_map/fold_couplings/pallas_call | solution.py:359
  22.3 0.2 collective-permute-start.1
  22.4 2.2 %fold_couplings.6.refs_2_ = bf16[16,32,512]{2,1,0:T(8,128)(2,1)S(1)} custom-call(s32[16]{0:T(128)S(1)} %copy-done.1, s32[128]{0:T(128)S(1)} %bitcast.4, s32[8,2048]{1,0:T(8,128)S(1)} %get-tuple-element.14.keys, bf16[128,16,2048]{2,1,0:T(8,128)(2,1)} %w.7), custom_call_target="tpu_custom_call" | custom-call | flops 4194304 | bytes 3145728 | tf_op jit(solution)/shard_map/fold_couplings/pallas_call | solution.py:359
  24.7 0.5 collective-permute-start.2
  25.2 2.2 %fold_couplings.7.refs_3_ = bf16[16,32,512]{2,1,0:T(8,128)(2,1)S(1)} custom-call(s32[16]{0:T(128)S(1)} %copy-done.1, s32[128]{0:T(128)S(1)} %bitcast.5, s32[8,2048]{1,0:T(8,128)S(1)} %get-tuple-element.14.keys, bf16[128,16,2048]{2,1,0:T(8,128)(2,1)} %w.7), custom_call_target="tpu_custom_call" | custom-call | flops 4194304 | bytes 3145728 | tf_op jit(solution)/shard_map/fold_couplings/pallas_call | solution.py:359
  27.4 0.2 collective-permute-start.3
  27.6 0.0 collective-permute-done.refs_4_
  27.6 0.0 copy-start.4
  27.6 0.0 collective-permute-done.1.refs_5_
  27.6 0.0 copy-start.5
  27.6 0.0 collective-permute-done.2.refs_6_
  27.6 0.8 %copy-done.4 = bf16[16,32,512]{2,1,0:T(8,128)(2,1)} copy-done((bf16[16,32,512]{2,1,0:T(8,128)(2,1)}, bf16[16,32,512]{2,1,0:T(8,128)(2,1)S(1)}, u32[]{:S(2)}) %copy-start.4) | copy-done | bytes 524312
  28.4 0.2 copy-done.5
  28.6 0.0 copy-start.6
  28.6 0.8 %copy-done.6 = bf16[16,32,512]{2,1,0:T(8,128)(2,1)} copy-done((bf16[16,32,512]{2,1,0:T(8,128)(2,1)}, bf16[16,32,512]{2,1,0:T(8,128)(2,1)S(1)}, u32[]{:S(2)}) %copy-start.6) | copy-done | bytes 524312
  29.4 0.1 collective-permute-done.3.refs_7_
  29.5 6.3 %all-to-all-done.t = bf16[16,128,256]{2,1,0:T(8,128)(2,1)S(1)} async-done(((bf16[16,128,256]{2,1,0:T(8,128)(2,1)}), bf16[16,128,256]{2,1,0:T(8,128)(2,1)S(1)}, u32[]{:S(2)}, u32[]{:S(2)}) %all-to-all-start) | async-done | bytes 1048608 | tf_op jit(solution)/shard_map/all_to_all | solution.py:335
  35.8 3.5 %multiply.1 = s16[8,272,128]{2,1,0:T(8,128)(2,1)S(1)} custom-call(s32[16,256]{1,0:T(8,128)S(1)} %get-tuple-element.15.label_k, s32[512,128]{1,0:T(8,128)S(1)} %get-tuple-element.16.label_kept, bf16[16,128,256]{2,1,0:T(8,128)(2,1)S(1)} %all-to-all-done.t, bf16[16,32,512]{2,1,0:T(8,128)(2,1)S(1)} %fold_couplings.4.refs_0_, ...), custom_call_target="tpu_custom_call" | custom-call | tf_op jit(solution)/shard_map/multiply/pallas_call | solution.py:383
  39.3 23.0 %all_to_all.10.parts = s16[8,272,128]{2,1,0:T(8,128)(2,1)S(1)} all-to-all(s16[8,272,128]{2,1,0:T(8,128)(2,1)S(1)} %multiply.1), channel_id=1, replica_groups={{0,2,4,6,8,10,12,14},{1,3,5,7,9,11,13,15},{16,18,20,22,24,26,28,30},{17..., dimensions={0} | all-to-all | bytes 1114112 | tf_op jit(solution)/shard_map/all_to_all | solution.py:400
  62.2 1.0 %unfold.1 = f32[64,2048]{1,0:T(8,128)} custom-call(s32[64,128]{1,0:T(8,128)S(1)} %get-tuple-element.13.label_out, s32[8,2048]{1,0:T(8,128)S(1)} %get-tuple-element.14.keys, s16[8,272,128]{2,1,0:T(8,128)(2,1)S(1)} %all_to_all.10.parts), custom_call_target="tpu_custom_call" | custom-call | tf_op jit(solution)/shard_map/unfold/pallas_call | solution.py:401
Async XLA Ops:
  5.4 30.3 %all-to-all-start = ((bf16[16,128,256]{2,1,0:T(8,128)(2,1)}), bf16[16,128,256]{2,1,0:T(8,128)(2,1)S(1)}, u32[]{:S(2)}, u32[]{:S(2)}) async-start(bf16[16,128,256]{2,1,0:T(8,128)(2,1)} %get-tuple-element.17), calls=%async_computation | async-start | bytes 2097152 | tf_op jit(solution)/shard_map/all_to_all | solution.py:335
  12.8 0.7 %copy-start = (s32[16]{0:T(128)S(1)}, s32[16]{0:T(128)}, u32[]{:S(2)}) copy-start(s32[16]{0:T(128)} %occ.9) | copy-start | bytes 196
  13.5 0.7 %copy-start.2 = (s32[8]{0:T(128)S(1)}, s32[8]{0:T(128)}, u32[]{:S(2)}) copy-start(s32[8]{0:T(128)} %sizes.1) | copy-start | bytes 100
  14.2 0.7 %copy-start.3 = (s32[2]{0:T(128)S(1)}, s32[2]{0:T(128)}, u32[]{:S(2)}) copy-start(s32[2]{0:T(128)} %j_irrep.1) | copy-start | bytes 28
  16.7 0.7 %copy-start.1 = (s32[16]{0:T(128)S(1)}, s32[16]{0:T(128)}, u32[]{:S(2)}) copy-start(s32[16]{0:T(128)} %occ.9) | copy-start | bytes 196
  19.6 8.0 %collective-permute-start = (bf16[16,32,512]{2,1,0:T(8,128)(2,1)S(1)}, bf16[16,32,512]{2,1,0:T(8,128)(2,1)S(1)}, u32[]{:S(2)}, u32[]{:S(2)}) collective-permute-start(bf16[16,32,512]{2,1,0:T(8,128)(2,1)S(1)} %fold_couplings.4.refs_0_), channel_id=1, source_target_pairs={{0,1},{1,0},{2,3},{3,2},{4,5},{5,4},{6,7},{7,6},{8,9},{9,8},{10,11... | collective-permute-start | bytes 1572872 | tf_op jit(solution)/shard_map/ppermute | solution.py:381
  22.3 5.3 %collective-permute-start.1 = (bf16[16,32,512]{2,1,0:T(8,128)(2,1)S(1)}, bf16[16,32,512]{2,1,0:T(8,128)(2,1)S(1)}, u32[]{:S(2)}, u32[]{:S(2)}) collective-permute-start(bf16[16,32,512]{2,1,0:T(8,128)(2,1)S(1)} %fold_couplings.5.refs_1_), channel_id=1, source_target_pairs={{0,1},{1,0},{2,3},{3,2},{4,5},{5,4},{6,7},{7,6},{8,9},{9,8},{10,11... | collective-permute-start | bytes 1572872 | tf_op jit(solution)/shard_map/ppermute | solution.py:381
  24.7 2.9 %collective-permute-start.2 = (bf16[16,32,512]{2,1,0:T(8,128)(2,1)S(1)}, bf16[16,32,512]{2,1,0:T(8,128)(2,1)S(1)}, u32[]{:S(2)}, u32[]{:S(2)}) collective-permute-start(bf16[16,32,512]{2,1,0:T(8,128)(2,1)S(1)} %fold_couplings.6.refs_2_), channel_id=1, source_target_pairs={{0,1},{1,0},{2,3},{3,2},{4,5},{5,4},{6,7},{7,6},{8,9},{9,8},{10,11... | collective-permute-start | bytes 1572872 | tf_op jit(solution)/shard_map/ppermute | solution.py:381
  27.4 2.1 %collective-permute-start.3 = (bf16[16,32,512]{2,1,0:T(8,128)(2,1)S(1)}, bf16[16,32,512]{2,1,0:T(8,128)(2,1)}, u32[]{:S(2)}, u32[]{:S(2)}) collective-permute-start(bf16[16,32,512]{2,1,0:T(8,128)(2,1)S(1)} %fold_couplings.7.refs_3_), channel_id=1, source_target_pairs={{0,1},{1,0},{2,3},{3,2},{4,5},{5,4},{6,7},{7,6},{8,9},{9,8},{10,11... | collective-permute-start | bytes 1572872 | tf_op jit(solution)/shard_map/ppermute | solution.py:381
  27.6 0.8 %copy-start.4 = (bf16[16,32,512]{2,1,0:T(8,128)(2,1)}, bf16[16,32,512]{2,1,0:T(8,128)(2,1)S(1)}, u32[]{:S(2)}) copy-start(bf16[16,32,512]{2,1,0:T(8,128)(2,1)S(1)} %collective-permute-done.refs_4_) | copy-start | bytes 1572868
  27.6 1.0 %copy-start.5 = (bf16[16,32,512]{2,1,0:T(8,128)(2,1)}, bf16[16,32,512]{2,1,0:T(8,128)(2,1)S(1)}, u32[]{:S(2)}) copy-start(bf16[16,32,512]{2,1,0:T(8,128)(2,1)S(1)} %collective-permute-done.1.refs_5_) | copy-start | bytes 1572868
  28.6 0.8 %copy-start.6 = (bf16[16,32,512]{2,1,0:T(8,128)(2,1)}, bf16[16,32,512]{2,1,0:T(8,128)(2,1)S(1)}, u32[]{:S(2)}) copy-start(bf16[16,32,512]{2,1,0:T(8,128)(2,1)S(1)} %collective-permute-done.2.refs_6_) | copy-start | bytes 1572868

commit v5 on v4

--- a/solution.py
+++ b/solution.py
@@ -14,6 +14,8 @@
 TOP = 32767.0
 STEPS = 256.0
 SMALL = 2.0**-126
+HALF = MOST // 2
+ALIGN = 16
 PAD = 16
 
 
@@ -56,26 +58,46 @@
     return start + iota((virtuals, 1), 0) % BS
 
 
+def wide_flags(partner, sizes):
+    wide = jnp.zeros_like(partner)
+    for h in range(sizes.shape[0]):
+        wide = jnp.where(partner == h, (sizes[h] > HALF).astype(I32), wide)
+    return wide
+
+
+def wide_block(block, wanted, sizes):
+    wide = jnp.zeros_like(block ^ wanted)
+    for r in range(BS):
+        wide = wide | wide_flags(irrep_of(block * BS + r, sizes) ^ wanted, sizes)
+    return wide
+
+
+def slots_needed(wide, owned):
+    return wide + (owned - wide + 1) // 2
+
+
+def slots_of(wide, rank, rank_wide, count_wide):
+    rank_narrow = rank - rank_wide
+    slot = jnp.where(wide == 1, rank_wide, count_wide + rank_narrow // 2)
+    return slot, jnp.where(wide == 1, 0, 1 + rank_narrow % 2)
+
+
 def pack_kernel(
-    rows,
     rows_out,
+    classes,
     sizes_hbm,
     occ_hbm,
     pair,
     owner_hbm,
     t_hbm,
-    out_hbm,
-    place,
-    sizes,
-    occ,
-    owner_row,
-    t_vmem,
-    out,
-    in_sems,
-    out_sems,
+    *refs,
 ):
+    outs, choice = refs[: len(classes)], refs[len(classes)]
+    sizes, occ, owner_row, t_vmem, folds, filled, out, in_sems, out_sems = refs[len(classes) + 1 :]
     virtuals = t_hbm.shape[1]
-    lanes = 2 * rows
+    blocks = owner_row.shape[1]
+    chips = outs[0].shape[0] // 2
+    quarter = HALF // 2
     pairs = (
         (owner_hbm, owner_row),
         (sizes_hbm, sizes),
@@ -89,53 +111,101 @@
     for copy in copies:
         copy.start()
     copies[0].wait()
-    where = block_place(owner_row[...], rows)
-    place[...] = jnp.broadcast_to(where, place.shape)
-    target = jnp.broadcast_to(virtual_place(where, virtuals), (virtuals, lanes))
+    chip_row = owner_row[...] // 2
+    first, second = iota((blocks, blocks), 0), iota((blocks, blocks), 1)
+    chip_col = jnp.sum(jnp.where(first == second, chip_row, 0), axis=1, keepdims=True)
+    same = chip_col == chip_row
+    before = jnp.where(same & (first < second), 1.0, 0.0).astype(BF16)
+    same = jnp.where(same, 1.0, 0.0).astype(BF16)
     for copy in copies[1:3]:
         copy.wait()
     wanted = pair[0] ^ occ[lax.axis_index("vir")]
-    label_e = irrep_of(iota((virtuals, 1), 0), sizes) ^ wanted
+    row = iota((8, blocks), 0)
+    wide_all = wide_block(iota((1, blocks), 1), row, sizes)
+    own = jnp.sum(jnp.where(row == wanted, wide_all, 0), axis=0, keepdims=True)
+    rest = jnp.where(row == 0, own, jnp.where(row == 1, 1, 0))
+    tallies = jnp.concatenate([wide_all, rest], axis=0).astype(F32).astype(BF16)
+    ahead = jnp.dot(tallies, before, preferred_element_type=F32).astype(I32)
+    total = jnp.dot(tallies, same, preferred_element_type=F32).astype(I32)
+    owned = total[9:10]
+
+    index = jnp.int32(0)
+    if len(classes) > 1:
+        used = jnp.int32(0)
+        for m in range(occ.shape[0]):
+            used = used | (jnp.int32(1) << (pair[0] ^ occ[m]))
+        need = slots_needed(total[:8], owned) * ((used >> row) & 1)
+        need = jnp.max(need) * BS
+        for size in classes[:-1]:
+            index = index + (need > size).astype(I32)
+    choice[0] = index
+
+    step = ALIGN // BS
+    chip = iota((chips, 1), 0)
+    lengths = jnp.where(chip == chip_row, slots_needed(total[8:9], owned), 0)
+    lengths = (jnp.max(lengths, axis=1, keepdims=True) + (step - 1)) // step
+    starts_row = jnp.sum(jnp.where(chip < chip_row, lengths, 0), axis=0, keepdims=True)
+    starts = [jnp.sum(jnp.where(chip < q, lengths, 0)) for q in range(chips)]
+    slot, kind = slots_of(own, ahead[9:10], ahead[8:9], total[8:9])
+    place = starts_row * step + slot
+    targets = [jnp.where(kind == 2, -1, place), jnp.where(kind == 1, -1, place)]
+
+    partner = irrep_of(iota((virtuals, 1), 0), sizes) ^ wanted
     label_a = irrep_of(iota((1, virtuals), 1), sizes)
     copies[3].wait()
-    folded = jnp.zeros((virtuals, MOST), F32)
-    for k in range(virtuals // MOST):
-        part = slice(k * MOST, (k + 1) * MOST)
-        folded = folded + jnp.where(
-            label_e == label_a[:, part], t_vmem[:, part].astype(F32), 0.0
+    halves = [jnp.zeros((virtuals, HALF), F32) for _ in range(2)]
+    for i, k in enumerate(range(0, virtuals, HALF)):
+        kept = jnp.where(partner == label_a[:, k : k + HALF], t_vmem[:, k : k + HALF].astype(F32), 0.0)
+        halves[i % 2] = halves[i % 2] + kept
+    for h in range(2):
+        folds[h] = halves[h]
+    first, second = iota((blocks, blocks), 0), iota((blocks, blocks), 1)
+    narrow = jnp.sum(jnp.where(first == second, own, 0), axis=1, keepdims=True) == 0
+    blank = jnp.zeros((blocks, quarter), F32)
+    sources = [[], []]
+    for r in range(BS):
+        both = [folds[h, pl.ds(r, blocks, stride=BS), :] for h in range(2)]
+        for h in range(2):
+            source = both[h] + jnp.where(narrow, both[1 - h], 0.0)
+            if rows_out < quarter:
+                old, new = iota((HALF, HALF), 0), iota((HALF, HALF), 1)
+                core, x = new // quarter, new % quarter
+                lane = x // rows_out * (2 * rows_out) + core * rows_out + x % rows_out
+                order = jnp.where(old == lane, 1.0, 0.0).astype(BF16)
+                source = jnp.dot(source.astype(BF16), order, preferred_element_type=F32)
+            for core in range(2):
+                side = source[:, core * quarter : (core + 1) * quarter]
+                sources[h] += [blank, side] if h else [side, blank]
+    sources = jnp.concatenate([jnp.concatenate(x, axis=1) for x in sources], axis=0).astype(BF16)
+    count = filled.shape[1] // BS
+    slot = iota((count, 1), 0)
+    hot = jnp.concatenate([jnp.where(x == slot, 1.0, 0.0) for x in targets], axis=1).astype(BF16)
+    moved = jnp.dot(hot, sources, preferred_element_type=F32)
+    for r in range(BS):
+        for core in range(2):
+            part = slice((2 * r + core) * HALF, (2 * r + core + 1) * HALF)
+            filled[core, pl.ds(r, count, stride=BS), :] = moved[:, part]
+    for core in range(2):
+        out[core, : filled.shape[1]] = filled[core].astype(BF16)
+        rest = out.shape[1] - filled.shape[1]
+        out[core, filled.shape[1] :] = jnp.zeros((rest, HALF), BF16)
+
+    def send(k, device):
+        start = pl.multiple_of(starts[device // 2] * ALIGN, ALIGN)
+        return pltpu.make_async_copy(
+            out.at[device % 2, pl.ds(start, classes[k])],
+            outs[k].at[device],
+            out_sems.at[device],
         )
-    folded_t = folded.T.astype(BF16)
-    lane = iota((1, lanes), 1)
-
-    def half(values, core):
-        return jnp.concatenate(
-            [
-                values[start : start + rows_out]
-                for start in range(core * rows_out, MOST, 2 * rows_out)
-            ],
-            axis=0,
-        )
-
-    sends = []
-    for chip in range(out.shape[0] // 2):
-
-        def moved(flip):
-            hot = jnp.where(target == (lane ^ flip) + chip * lanes, 1.0, 0.0).astype(BF16)
-            return jnp.dot(folded_t, hot, preferred_element_type=F32)
-
-        here = moved(0)
-        out[2 * chip] = half(here, 0).astype(BF16)
-        if rows % 128 == 0:
-            there = half(here, 1)
-            out[2 * chip + 1, :, :rows] = there[:, rows:].astype(BF16)
-            out[2 * chip + 1, :, rows:] = there[:, :rows].astype(BF16)
-        else:
-            out[2 * chip + 1] = half(moved(rows), 1).astype(BF16)
-        both = pl.ds(2 * chip, 2)
-        sends.append(pltpu.make_async_copy(out.at[both], out_hbm.at[both], out_sems.at[chip]))
-        sends[-1].start()
-    for copy in sends:
-        copy.wait()
+
+    for k in range(len(classes)):
+
+        @pl.when(index == k)
+        def _(k=k):
+            for device in range(2 * chips):
+                send(k, device).start()
+            for device in range(2 * chips):
+                send(k, device).wait()
 
 
 def label_kernel(
@@ -145,24 +215,45 @@
     occ,
     pair,
     j_irrep,
-    place,
+    owner_row,
     label_row,
     label_k,
+    slots,
+    kinds,
     label_kept,
     label_out,
     keys,
 ):
     here = lax.axis_index("vir")
     occupied, lanes = label_k.shape
-    virtuals = place.shape[1] * BS
-    target = virtual_place(place[:1, :], virtuals)
+    virtuals = owner_row.shape[1] * BS
+    target = virtual_place(block_place(owner_row[...], rows), virtuals)
     lane = iota((virtuals, lanes), 1)
     source = jnp.where(lane < rows, lane + here * rows, lane - rows + (here ^ 1) * rows)
-    label_e = irrep_of(iota((virtuals, 1), 0), sizes)
-    label = jnp.sum(jnp.where(target == source, label_e, 0), axis=0, keepdims=True)
+    virtual = iota((virtuals, lanes), 0)
+    e_row = jnp.sum(jnp.where(target == source, virtual + 1, 0), axis=0, keepdims=True) - 1
+    label = irrep_of(e_row, sizes)
     label_row[...] = label[:, :rows]
+    m_row = iota((occupied, 1), 0)
+    wanted = jnp.zeros((occupied, 1), I32)
     for m in range(occupied):
-        label_k[m : m + 1, :] = label ^ (pair[0] ^ occ[m])
+        wanted = jnp.where(m_row == m, pair[0] ^ occ[m], wanted)
+    partner = label ^ wanted
+    label_k[...] = partner
+    first, second = iota((lanes, lanes), 0), iota((lanes, lanes), 1)
+    e_col = jnp.sum(jnp.where(first == second, e_row, 0), axis=1, keepdims=True)
+    ahead = (e_col >= 0) & (e_col % BS == 0) & (e_col // BS < e_row // BS)
+    wide = jnp.where(e_row >= 0, wide_block(jnp.maximum(e_row, 0) // BS, wanted, sizes), 0)
+    rank_wide = jnp.dot(
+        wide.astype(F32).astype(BF16),
+        jnp.where(ahead, 1.0, 0.0).astype(BF16),
+        preferred_element_type=F32,
+    ).astype(I32)
+    rank = jnp.sum(ahead.astype(I32), axis=0, keepdims=True)
+    count_wide = jnp.sum(wide, axis=1, keepdims=True) // BS
+    slot, kind = slots_of(wide, rank, rank_wide, count_wide)
+    slots[...] = jnp.where(e_row >= 0, slot * BS + e_row % BS, -1)
+    kinds[...] = kind
     row = iota(label_kept.shape, 0)
     a = row // rows_out * (2 * rows_out) + here % 2 * rows_out + row % rows_out
     label_kept[...] = irrep_of(a, sizes)
@@ -194,9 +285,9 @@
             ].astype(BF16)
 
 
-def product_kernel(pieces, label_k, label_kept, t, *refs):
+def product_kernel(pieces, label_k, slots, kinds, label_kept, packed, *refs):
     own, mate_hbm = refs[:pieces], refs[pieces : 2 * pieces]
-    coded, out, mate, sems = refs[2 * pieces :]
+    coded, out, t, mate, sems = refs[2 * pieces :]
     occupied, half, lanes = t.shape
     rows = lanes // 2
     kept = out.shape[0]
@@ -207,6 +298,23 @@
     ]
     for copy in copies:
         copy.start()
+    slot = iota((packed.shape[1], 1), 0)
+    unpacked = max(1, min(occupied, 8))
+
+    @pl.loop(0, occupied // unpacked)
+    def _(step):
+        for i in range(unpacked):
+            m = step * unpacked + i
+            hot = jnp.where(slots[pl.ds(m, 1), :] == slot, 1.0, 0.0).astype(BF16)
+            both = lax.dot_general(
+                packed[m], hot, (((0,), (0,)), ((), ())), preferred_element_type=F32
+            )
+            low, high = both[: half // 2], both[half // 2 :]
+            kind = kinds[pl.ds(m, 1), :]
+            t[m] = jnp.concatenate(
+                [jnp.where(kind == 2, high, low), jnp.where(kind == 1, low, high)], axis=0
+            ).astype(BF16)
+
     wide_label = jnp.broadcast_to(label_kept[:, :1], (kept, rows))
     out[...] = jnp.zeros(out.shape, F32)
     m_block = max(1, min(occupied, 1024 // rows))
@@ -306,22 +414,26 @@
     hbm = pl.BlockSpec(memory_space=pltpu.HBM)
     params = pltpu.CompilerParams(vmem_limit_bytes=LIMIT)
 
-    outgoing, place = pl.pallas_call(
-        functools.partial(pack_kernel, rows, rows_out),
-        out_shape=(
-            pltpu.HBM((devices, MOST // 2, lanes), BF16),
-            jax.ShapeDtypeStruct((8, blocks), I32),
-        ),
+    classes = [lanes]
+    if lanes % 256 == 0:
+        classes = [lanes // 16 * part for part in (10, 11, 12, 13, 16)]
+    owner_row = owner.reshape(1, blocks)
+    *outgoing, choice = pl.pallas_call(
+        functools.partial(pack_kernel, rows_out, classes),
+        out_shape=[jax.ShapeDtypeStruct((devices, size, HALF), BF16) for size in classes]
+        + [jax.ShapeDtypeStruct((1,), I32)],
         in_specs=[hbm, hbm, smem, hbm, hbm],
-        out_specs=(hbm, vmem),
+        out_specs=[hbm] * len(classes) + [smem],
         scratch_shapes=[
             pltpu.SMEM(block_sizes.shape, I32),
             pltpu.SMEM(occ_irrep.shape, I32),
             pltpu.VMEM((1, blocks), I32),
             pltpu.VMEM((virtuals, virtuals), BF16),
-            pltpu.VMEM((devices, MOST // 2, lanes), BF16),
+            pltpu.VMEM((2, virtuals, HALF), F32),
+            pltpu.VMEM((2, virtuals + chips * ALIGN, HALF), F32),
+            pltpu.VMEM((2, virtuals + chips * ALIGN + lanes, HALF), BF16),
             pltpu.SemaphoreType.DMA((4,)),
-            pltpu.SemaphoreType.DMA((chips,)),
+            pltpu.SemaphoreType.DMA((devices,)),
         ],
         compiler_params=params,
         name="pack_amplitudes",
@@ -329,83 +441,93 @@
         in_hbm(block_sizes),
         in_hbm(occ_irrep),
         pair_irrep,
-        in_hbm(owner.reshape(1, blocks)),
+        in_hbm(owner_row),
         in_hbm(amplitudes),
     )
-    received = lax.all_to_all(outgoing, "vir", 0, 0)
-
-    label_row, label_k, label_kept, label_out, keys = pl.pallas_call(
-        functools.partial(label_kernel, rows, rows_out),
-        out_shape=(
-            jax.ShapeDtypeStruct((1, rows), I32),
-            jax.ShapeDtypeStruct((occupied, lanes), I32),
-            jax.ShapeDtypeStruct((kept, 128), I32),
-            jax.ShapeDtypeStruct((rows_out, 128), I32),
-            jax.ShapeDtypeStruct((8, columns), I32),
-        ),
-        in_specs=[smem] * 4 + [vmem],
-        out_specs=(vmem,) * 5,
-        compiler_params=params,
-        name="labels",
-    )(block_sizes, occ_irrep, pair_irrep, j_irrep, place)
-
-    row_block, m_block = 16, 16
-    pieces = max(1, rows // 32)
-    piece_rows = rows // pieces
-    w_own, w_mate = [], []
-    for piece in range(pieces):
-        first = piece * piece_rows
-        w_own.append(
-            pl.pallas_call(
-                functools.partial(fold_kernel, first),
-                out_shape=jax.ShapeDtypeStruct((occupied, piece_rows, wide), BF16),
-                grid=(piece_rows // row_block, occupied // m_block),
-                in_specs=[smem, smem, vmem]
-                + [
-                    pl.BlockSpec(
-                        (row_block, m_block, columns),
-                        lambda i, j, skip=first // row_block: (skip + i, j, 0),
-                    )
-                ],
-                out_specs=pl.BlockSpec((m_block, row_block, wide), lambda i, j: (j, i, 0)),
-                scratch_shapes=[pltpu.VMEM((wide // 128, row_block * m_block, 128), F32)],
-                compiler_params=params,
-                cost_estimate=pl.CostEstimate(
-                    flops=4 * piece_rows * occupied * columns,
-                    bytes_accessed=3 * piece_rows * occupied * columns,
-                    transcendentals=0,
-                ),
-                name="fold_couplings",
-            )(occ_irrep, label_row.reshape(rows), keys, in_hbm(couplings))
+
+    def contract(packed):
+        received = lax.all_to_all(packed, "vir", 0, 0)
+
+        label_row, label_k, slots, kinds, label_kept, label_out, keys = pl.pallas_call(
+            functools.partial(label_kernel, rows, rows_out),
+            out_shape=(
+                jax.ShapeDtypeStruct((1, rows), I32),
+                jax.ShapeDtypeStruct((occupied, lanes), I32),
+                jax.ShapeDtypeStruct((occupied, lanes), I32),
+                jax.ShapeDtypeStruct((occupied, lanes), I32),
+                jax.ShapeDtypeStruct((kept, 128), I32),
+                jax.ShapeDtypeStruct((rows_out, 128), I32),
+                jax.ShapeDtypeStruct((8, columns), I32),
+            ),
+            in_specs=[smem] * 4 + [vmem],
+            out_specs=(vmem,) * 7,
+            compiler_params=params,
+            name="labels",
+        )(block_sizes, occ_irrep, pair_irrep, j_irrep, owner_row)
+
+        row_block, m_block = 16, 16
+        pieces = max(1, rows // 32)
+        piece_rows = rows // pieces
+        w_own, w_mate = [], []
+        for piece in range(pieces):
+            first = piece * piece_rows
+            w_own.append(
+                pl.pallas_call(
+                    functools.partial(fold_kernel, first),
+                    out_shape=jax.ShapeDtypeStruct((occupied, piece_rows, wide), BF16),
+                    grid=(piece_rows // row_block, occupied // m_block),
+                    in_specs=[smem, smem, vmem]
+                    + [
+                        pl.BlockSpec(
+                            (row_block, m_block, columns),
+                            lambda i, j, skip=first // row_block: (skip + i, j, 0),
+                        )
+                    ],
+                    out_specs=pl.BlockSpec((m_block, row_block, wide), lambda i, j: (j, i, 0)),
+                    scratch_shapes=[pltpu.VMEM((wide // 128, row_block * m_block, 128), F32)],
+                    compiler_params=params,
+                    cost_estimate=pl.CostEstimate(
+                        flops=4 * piece_rows * occupied * columns,
+                        bytes_accessed=3 * piece_rows * occupied * columns,
+                        transcendentals=0,
+                    ),
+                    name="fold_couplings",
+                )(occ_irrep, label_row.reshape(rows), keys, in_hbm(couplings))
+            )
+            w_mate.append(lax.ppermute(w_own[-1], "vir", [(d, d ^ 1) for d in range(devices)]))
+
+        partial = pl.pallas_call(
+            functools.partial(product_kernel, pieces),
+            out_shape=jax.ShapeDtypeStruct((chips, wide // 128 * rows_out + PAD, 128), I16),
+            in_specs=[vmem] * (5 + pieces) + [hbm] * pieces,
+            out_specs=vmem,
+            scratch_shapes=[
+                pltpu.VMEM((kept, wide), F32),
+                pltpu.VMEM((occupied, HALF, lanes), BF16),
+                pltpu.VMEM((occupied, rows, wide), BF16),
+                pltpu.SemaphoreType.DMA((pieces,)),
+            ],
+            compiler_params=params,
+            name="multiply",
+        )(
+            *[in_vmem(x) for x in (label_k, slots, kinds, label_kept, received, *w_own)],
+            *[in_hbm(x) for x in w_mate],
         )
-        w_mate.append(lax.ppermute(w_own[-1], "vir", [(d, d ^ 1) for d in range(devices)]))
-
-    partial = pl.pallas_call(
-        functools.partial(product_kernel, pieces),
-        out_shape=jax.ShapeDtypeStruct((chips, wide // 128 * rows_out + PAD, 128), I16),
-        in_specs=[vmem] * (3 + pieces) + [hbm] * pieces,
-        out_specs=vmem,
-        scratch_shapes=[
-            pltpu.VMEM((kept, wide), F32),
-            pltpu.VMEM((occupied, rows, wide), BF16),
-            pltpu.SemaphoreType.DMA((pieces,)),
-        ],
-        compiler_params=params,
-        name="multiply",
-    )(
-        *[in_vmem(x) for x in (label_k, label_kept, received, *w_own)],
-        *[in_hbm(x) for x in w_mate],
-    )
-    sides = [[d for d in range(devices) if d % 2 == core] for core in (0, 1)]
-    parts = lax.all_to_all(partial, "vir", 0, 0, axis_index_groups=sides)
-    return pl.pallas_call(
-        finish_kernel,
-        out_shape=jax.ShapeDtypeStruct((rows_out, columns), F32),
-        in_specs=[vmem] * 3,
-        out_specs=vmem,
-        compiler_params=params,
-        name="unfold",
-    )(label_out, keys, parts)
+        sides = [[d for d in range(devices) if d % 2 == core] for core in (0, 1)]
+        parts = lax.all_to_all(partial, "vir", 0, 0, axis_index_groups=sides)
+        return pl.pallas_call(
+            finish_kernel,
+            out_shape=pltpu.HBM((rows_out, columns), F32),
+            in_specs=[vmem] * 3,
+            out_specs=vmem,
+            compiler_params=params,
+            name="unfold",
+        )(label_out, keys, parts)
+
+    if len(classes) == 1:
+        return contract(outgoing[0])
+    branches = [lambda *packed, k=k: contract(packed[k]) for k in range(len(classes))]
+    return lax.switch(choice[0], branches, *outgoing)
 
 
 def solution(mesh):

time: 63.6 us -> 64.8 us (1.019)
  the two profiles are of different devices: /device:TPU:0 before, /device:TPU:2 now
where the time goes in v5:
time: 64.8 us; the launch traced here: 64.4 us
  blocking collectives  23 us (35%)
  Pallas kernels  22.2 us (34%)
  waiting for transfers between devices  8.35 us (13%)
  starting transfers between devices  7.23 us (11%)
  local copies, waits for them, and re-layouts  1.75 us (3%)
  between operations  1.31 us (2%)
    all_to_all x1, blocking collectives, contract(): parts = lax.all_to_all(partial, 'vir', 0, 0, axis_index_groups=sides)  23 us
    pallas_call x4, Pallas kernels, contract(): pl.pallas_call(functools.partial(fold_kernel, first), out_shape=jax.Shape...  8.95 us
    all_to_all x1, waiting for transfers between devices, contract(): received = lax.all_to_all(packed, 'vir', 0, 0)  8.17 us
    all_to_all x1, starting transfers between devices, contract(): received = lax.all_to_all(packed, 'vir', 0, 0)  5.95 us
    pallas_call x1, Pallas kernels, per_device(): pl.pallas_call(functools.partial(pack_kernel, rows_out, classes), out_sha...  5.42 us
    pallas_call x1, Pallas kernels, contract(): pl.pallas_call(functools.partial(product_kernel, pieces), out_shape=jax.S...  4.22 us
    pallas_call x1, Pallas kernels, contract(): pl.pallas_call(functools.partial(label_kernel, rows, rows_out), out_shape...  2.55 us
    cond x10, local copies, waits for them, and re-layouts  1.75 us
  transfers between devices with their start and end apart: 5, of which 2 were waited for; matrix products, arithmetic and copies ran while one was open for 0% of the time, Pallas kernels for 18%

profile of v5, /device:TPU:2, one launch (start us, length us, event | category | flops | bytes accessed | tf_op | source)
XLA Modules:
  0.0 64.4 jit_solution(7792408788661890174)
XLA Ops:
  0.7 5.4 %pack_amplitudes.1 = (bf16[16,160,128]{2,1,0:T(8,128)(2,1)}, bf16[16,176,128]{2,1,0:T(8,128)(2,1)}, bf16[16,192,128]{2,1,0:T(8,128)(2,1)}, bf16[16,208,128]{2,1,...) custom-call(s32[8]{0:T(128)} %sizes_hbm.1, s32[16]{0:T(128)} %occ_hbm.1, s32[1]{0:T(128)S(6)} %copy.18.pair, ...), custom_call_target="tpu_custom_call" | custom-call | tf_op jit(solution)/shard_map/pack_amplitudes/pallas_call | solution.py:421
  6.7 57.7 %conditional.1 = (f32[64,2048]{1,0:T(8,128)}) conditional(s32[]{:T(128)} %bitcast.6, (s32[8]{0:T(128)}, s32[16]{0:T(128)}, s32[1]{0:T(128)}, s32[2]{0:T(128)}, s32[1,256]{1,0:T(1,128)}, /*index=5*/bf16[16,160,128]{2,1,0:T(8,128)(2,1)}, bf16[128,16,2048]{2,1,0:T(8,128)(2,1)}) %tuple.35, (s32[8]{0:T(128)}, ...), branch_computations={%region_0.0_spmd, %region_1.0_spmd, %region_2.0_spmd, %region_3.0_... | conditional | flops 16777216 | bytes 31523668 | solution.py:530
  7.3 0.0 copy-start.19
  7.3 5.9 %all-to-all-start.8 = ((bf16[16,256,128]{2,1,0:T(8,128)(2,1)}), bf16[16,256,128]{2,1,0:T(8,128)(2,1)S(1)}, u32[]{:S(2)}, u32[]{:S(2)}) async-start(bf16[16,256,128]{2,1,0:T(8,128)(2,1)} %get-tuple-element.148), calls=%async_computation.8 | async-start | bytes 2097152 | tf_op jit(solution)/shard_map/cond/branch_4_fun/all_to_all | solution.py:449
  13.2 2.6 %labels.9 = (s32[1,128]{1,0:T(1,128)S(1)}, s32[16,256]{1,0:T(8,128)S(1)}, s32[16,256]{1,0:T(8,128)S(1)}, s32[16,256]{1,0:T(8,128)S(1)}, s32[512,128]{1,0:T(8,128...) custom-call(s32[8]{0:T(128)} %get-tuple-element.137.sizes, s32[16]{0:T(128)} %get-tuple-element.138.occ, ...), custom_call_target="tpu_custom_call" | custom-call | tf_op jit(solution)/shard_map/cond/branch_4_fun/labels/pallas_call | solution.py:451
  15.8 2.2 %fold_couplings.36.refs_0_ = bf16[16,32,512]{2,1,0:T(8,128)(2,1)S(1)} custom-call(s32[16]{0:T(128)} %get-tuple-element.138.occ, s32[128]{0:T(128)S(1)} %bitcast.23, s32[8,2048]{1,0:T(8,128)S(1)} %get-tuple-element.143.keys, bf16[128,16,2048]{2,1,0:T(8,128)(2,1)} %get-tuple-element.150.w), custom_call_target="tpu_custom_call" | custom-call | flops 4194304 | bytes 3145728 | tf_op jit(solution)/shard_map/cond/branch_4_fun/fold_couplings/pallas_call | solution.py:475
  18.0 0.0 copy-start.20
  18.0 0.5 collective-permute-start.16
  18.5 0.0 copy-done.19
  18.5 2.2 %fold_couplings.37.refs_1_ = bf16[16,32,512]{2,1,0:T(8,128)(2,1)S(1)} custom-call(s32[16]{0:T(128)S(1)} %copy-done.19, s32[128]{0:T(128)S(1)} %bitcast.24, s32[8,2048]{1,0:T(8,128)S(1)} %get-tuple-element.143.keys, bf16[128,16,2048]{2,1,0:T(8,128)(2,1)} %get-tuple-element.150.w), custom_call_target="tpu_custom_call" | custom-call | flops 4194304 | bytes 3145728 | tf_op jit(solution)/shard_map/cond/branch_4_fun/fold_couplings/pallas_call | solution.py:475
  20.8 0.2 collective-permute-start.17
  20.9 2.2 %fold_couplings.38.refs_2_ = bf16[16,32,512]{2,1,0:T(8,128)(2,1)S(1)} custom-call(s32[16]{0:T(128)S(1)} %copy-done.19, s32[128]{0:T(128)S(1)} %bitcast.25, s32[8,2048]{1,0:T(8,128)S(1)} %get-tuple-element.143.keys, bf16[128,16,2048]{2,1,0:T(8,128)(2,1)} %get-tuple-element.150.w), custom_call_target="tpu_custom_call" | custom-call | flops 4194304 | bytes 3145728 | tf_op jit(solution)/shard_map/cond/branch_4_fun/fold_couplings/pallas_call | solution.py:475
  23.2 0.5 collective-permute-start.18
  23.6 0.0 copy-done.20
  23.6 2.2 %fold_couplings.39.refs_3_ = bf16[16,32,512]{2,1,0:T(8,128)(2,1)S(1)} custom-call(s32[16]{0:T(128)S(1)} %copy-done.20, s32[128]{0:T(128)S(1)} %bitcast.26, s32[8,2048]{1,0:T(8,128)S(1)} %get-tuple-element.143.keys, bf16[128,16,2048]{2,1,0:T(8,128)(2,1)} %get-tuple-element.150.w), custom_call_target="tpu_custom_call" | custom-call | flops 4194304 | bytes 3145728 | tf_op jit(solution)/shard_map/cond/branch_4_fun/fold_couplings/pallas_call | solution.py:475
  25.9 0.2 collective-permute-start.19
  26.1 0.0 collective-permute-done.16.refs_4_
  26.1 0.0 copy-start.2
  26.1 0.0 collective-permute-done.17.refs_5_
  26.1 0.0 copy-start.5
  26.1 0.0 collective-permute-done.18.refs_6_
  26.1 0.8 %copy-done.2 = bf16[16,32,512]{2,1,0:T(8,128)(2,1)} copy-done((bf16[16,32,512]{2,1,0:T(8,128)(2,1)}, bf16[16,32,512]{2,1,0:T(8,128)(2,1)S(1)}, u32[]{:S(2)}) %copy-start.2) | copy-done | bytes 524312 | tf_op jit(solution)/shard_map/cond
  26.9 0.2 copy-done.5
  27.0 0.0 copy-start.8
  27.0 0.8 %copy-done.8 = bf16[16,32,512]{2,1,0:T(8,128)(2,1)} copy-done((bf16[16,32,512]{2,1,0:T(8,128)(2,1)}, bf16[16,32,512]{2,1,0:T(8,128)(2,1)S(1)}, u32[]{:S(2)}) %copy-start.8) | copy-done | bytes 524312 | tf_op jit(solution)/shard_map/cond
  27.8 0.2 collective-permute-done.19.refs_7_
  28.0 8.2 %all-to-all-done.8.packed = bf16[16,256,128]{2,1,0:T(8,128)(2,1)S(1)} async-done(((bf16[16,256,128]{2,1,0:T(8,128)(2,1)}), bf16[16,256,128]{2,1,0:T(8,128)(2,1)S(1)}, u32[]{:S(2)}, u32[]{:S(2)}) %all-to-all-start.8) | async-done | bytes 1048608 | tf_op jit(solution)/shard_map/cond/branch_4_fun/all_to_all | solution.py:449
  36.2 4.2 %multiply.9 = s16[8,272,128]{2,1,0:T(8,128)(2,1)S(1)} custom-call(s32[16,256]{1,0:T(8,128)S(1)} %get-tuple-element.144.label_k, s32[16,256]{1,0:T(8,128)S(1)} %get-tuple-element.145.slots, s32[16,256]{1,0:T(8,128)S(1)} %get-tuple-element.146.kinds, s32[512,128]{1,0:T(8,128)S(1)} %get-tuple-element.147.label_kept, ...), custom_call_target="tpu_custom_call" | custom-call | tf_op jit(solution)/shard_map/cond/branch_4_fun/multiply/pallas_call | solution.py:499
  40.4 23.0 %all_to_all.44.parts = s16[8,272,128]{2,1,0:T(8,128)(2,1)S(1)} all-to-all(s16[8,272,128]{2,1,0:T(8,128)(2,1)S(1)} %multiply.9), channel_id=1, replica_groups={{0,2,4,6,8,10,12,14},{1,3,5,7,9,11,13,15},{16,18,20,22,24,26,28,30},{17..., dimensions={0} | all-to-all | bytes 1114112 | tf_op jit(solution)/shard_map/cond/branch_4_fun/all_to_all | solution.py:517
  63.4 1.0 %unfold.9 = f32[64,2048]{1,0:T(8,128)} custom-call(s32[64,128]{1,0:T(8,128)S(1)} %get-tuple-element.142.label_out, s32[8,2048]{1,0:T(8,128)S(1)} %get-tuple-element.143.keys, s16[8,272,128]{2,1,0:T(8,128)(2,1)S(1)} %all_to_all.44.parts), custom_call_target="tpu_custom_call" | custom-call | tf_op jit(solution)/shard_map/cond/branch_4_fun/unfold/pallas_call | solution.py:518
Async XLA Ops:
  7.3 11.3 %copy-start.19 = (s32[16]{0:T(128)S(1)}, s32[16]{0:T(128)}, u32[]{:S(2)}) copy-start(s32[16]{0:T(128)} %get-tuple-element.138.occ) | copy-start | bytes 196 | tf_op jit(solution)/shard_map/cond
  7.3 28.9 %all-to-all-start.8 = ((bf16[16,256,128]{2,1,0:T(8,128)(2,1)}), bf16[16,256,128]{2,1,0:T(8,128)(2,1)S(1)}, u32[]{:S(2)}, u32[]{:S(2)}) async-start(bf16[16,256,128]{2,1,0:T(8,128)(2,1)} %get-tuple-element.148), calls=%async_computation.8 | async-start | bytes 2097152 | tf_op jit(solution)/shard_map/cond/branch_4_fun/all_to_all | solution.py:449
  18.0 5.6 %copy-start.20 = (s32[16]{0:T(128)S(1)}, s32[16]{0:T(128)}, u32[]{:S(2)}) copy-start(s32[16]{0:T(128)} %get-tuple-element.138.occ) | copy-start | bytes 196 | tf_op jit(solution)/shard_map/cond
  18.0 8.0 %collective-permute-start.16 = (bf16[16,32,512]{2,1,0:T(8,128)(2,1)S(1)}, bf16[16,32,512]{2,1,0:T(8,128)(2,1)S(1)}, u32[]{:S(2)}, u32[]{:S(2)}) collective-permute-start(bf16[16,32,512]{2,1,0:T(8,128)(2,1)S(1)} %fold_couplings.36.refs_0_), channel_id=1, source_target_pairs={{0,1},{1,0},{2,3},{3,2},{4,5},{5,4},{6,7},{7,6},{8,9},{9,8},{10,11... | collective-permute-start | bytes 1572872 | tf_op jit(solution)/shard_map/cond/branch_4_fun/ppermute | solution.py:497
  20.8 5.3 %collective-permute-start.17 = (bf16[16,32,512]{2,1,0:T(8,128)(2,1)S(1)}, bf16[16,32,512]{2,1,0:T(8,128)(2,1)S(1)}, u32[]{:S(2)}, u32[]{:S(2)}) collective-permute-start(bf16[16,32,512]{2,1,0:T(8,128)(2,1)S(1)} %fold_couplings.37.refs_1_), channel_id=1, source_target_pairs={{0,1},{1,0},{2,3},{3,2},{4,5},{5,4},{6,7},{7,6},{8,9},{9,8},{10,11... | collective-permute-start | bytes 1572872 | tf_op jit(solution)/shard_map/cond/branch_4_fun/ppermute | solution.py:497
  23.2 2.9 %collective-permute-start.18 = (bf16[16,32,512]{2,1,0:T(8,128)(2,1)S(1)}, bf16[16,32,512]{2,1,0:T(8,128)(2,1)S(1)}, u32[]{:S(2)}, u32[]{:S(2)}) collective-permute-start(bf16[16,32,512]{2,1,0:T(8,128)(2,1)S(1)} %fold_couplings.38.refs_2_), channel_id=1, source_target_pairs={{0,1},{1,0},{2,3},{3,2},{4,5},{5,4},{6,7},{7,6},{8,9},{9,8},{10,11... | collective-permute-start | bytes 1572872 | tf_op jit(solution)/shard_map/cond/branch_4_fun/ppermute | solution.py:497
  25.9 2.1 %collective-permute-start.19 = (bf16[16,32,512]{2,1,0:T(8,128)(2,1)S(1)}, bf16[16,32,512]{2,1,0:T(8,128)(2,1)}, u32[]{:S(2)}, u32[]{:S(2)}) collective-permute-start(bf16[16,32,512]{2,1,0:T(8,128)(2,1)S(1)} %fold_couplings.39.refs_3_), channel_id=1, source_target_pairs={{0,1},{1,0},{2,3},{3,2},{4,5},{5,4},{6,7},{7,6},{8,9},{9,8},{10,11... | collective-permute-start | bytes 1572872 | tf_op jit(solution)/shard_map/cond/branch_4_fun/ppermute | solution.py:497
  26.1 0.8 %copy-start.2 = (bf16[16,32,512]{2,1,0:T(8,128)(2,1)}, bf16[16,32,512]{2,1,0:T(8,128)(2,1)S(1)}, u32[]{:S(2)}) copy-start(bf16[16,32,512]{2,1,0:T(8,128)(2,1)S(1)} %collective-permute-done.16.refs_4_) | copy-start | bytes 1572868 | tf_op jit(solution)/shard_map/cond
  26.1 1.0 %copy-start.5 = (bf16[16,32,512]{2,1,0:T(8,128)(2,1)}, bf16[16,32,512]{2,1,0:T(8,128)(2,1)S(1)}, u32[]{:S(2)}) copy-start(bf16[16,32,512]{2,1,0:T(8,128)(2,1)S(1)} %collective-permute-done.17.refs_5_) | copy-start | bytes 1572868 | tf_op jit(solution)/shard_map/cond
  27.0 0.8 %copy-start.8 = (bf16[16,32,512]{2,1,0:T(8,128)(2,1)}, bf16[16,32,512]{2,1,0:T(8,128)(2,1)S(1)}, u32[]{:S(2)}) copy-start(bf16[16,32,512]{2,1,0:T(8,128)(2,1)S(1)} %collective-permute-done.18.refs_6_) | copy-start | bytes 1572868 | tf_op jit(solution)/shard_map/cond
